TPU v7x, 32 devices: a whole 2x2x4 slice. The times are simulated.
32 devices in a mesh: rep: 8 (over z, y), shard: 4 (over x, core).
Axes of the slice: x: 2, y: 2, z: 4, core: 2. Of those that a mesh axis runs over, the one named last changes fastest.
Arguments:
- tokens: bfloat16 [16, 1024, 1536], P('rep', 'shard'), may hold values from -6 to 6
- cotangent: bfloat16 [16, 1024, 1536], P('rep', 'shard'), may hold values from -6 to 6
- prefix_len: int32 [16], P('rep'), may hold values from 102 to 512
- adapter_index: int32 [16], P('rep'), may hold values from 0 to 7
- gain_attn: bfloat16 [1536], replicated, may hold values from 0.099609375 to 1.8984375
- gain_mlp: bfloat16 [1536], replicated, may hold values from 0.099609375 to 1.8984375
- query_weight: bfloat16 [1536, 1536], P('shard'), may hold values from -0.15625 to 0.15625
- key_weight: bfloat16 [1536, 768], P('shard'), may hold values from -0.15625 to 0.15625
- value_weight: bfloat16 [1536, 768], P('shard'), may hold values from -0.15625 to 0.15625
- output_weight: bfloat16 [1536, 1536], P('shard'), may hold values from -2.5 to 2.5
- gate_weight: bfloat16 [1536, 4096], P('shard'), may hold values from -0.15625 to 0.15625
- lift_weight: bfloat16 [1536, 4096], P('shard'), may hold values from -0.15625 to 0.15625
- drop_weight: bfloat16 [4096, 1536], P('shard'), may hold values from -0.09375 to 0.09375
- query_inner: bfloat16 [1536, 128], P('shard'), may hold values from -0.15625 to 0.15625
- query_outer: bfloat16 [128, 1536], P(None, 'shard'), may hold values from -0.75 to 0.75
- key_inner: bfloat16 [1536, 128], P('shard'), may hold values from -0.15625 to 0.15625
- key_outer: bfloat16 [128, 768], P(None, 'shard'), may hold values from -0.75 to 0.75
- value_inner: bfloat16 [1536, 128], P('shard'), may hold values from -0.15625 to 0.15625
- value_outer: bfloat16 [128, 768], P(None, 'shard'), may hold values from -0.75 to 0.75
- output_inner: bfloat16 [1536, 128], P('shard'), may hold values from -2.5 to 2.5
- output_outer: bfloat16 [128, 1536], P(None, 'shard'), may hold values from -0.75 to 0.75
- gate_inner: bfloat16 [1536, 128], P('shard'), may hold values from -0.15625 to 0.15625
- gate_outer: bfloat16 [128, 4096], P(None, 'shard'), may hold values from -0.75 to 0.75
- lift_inner: bfloat16 [1536, 128], P('shard'), may hold values from -0.15625 to 0.15625
- lift_outer: bfloat16 [128, 4096], P(None, 'shard'), may hold values from -0.75 to 0.75
- drop_inner: bfloat16 [4096, 128], P('shard'), may hold values from -0.09375 to 0.09375
- drop_outer: bfloat16 [128, 1536], P(None, 'shard'), may hold values from -0.75 to 0.75
Outputs:
- mixed: bfloat16 [16, 1024, 1536], P('rep', 'shard')
- input_grad: float32 [16, 1024, 1536], P('rep', 'shard')
- query_inner_grad: float32 [1536, 128], P('shard')
- query_outer_grad: float32 [128, 1536], P(None, 'shard')
- key_inner_grad: float32 [1536, 128], P('shard')
- key_outer_grad: float32 [128, 768], P(None, 'shard')
- value_inner_grad: float32 [1536, 128], P('shard')
- value_outer_grad: float32 [128, 768], P(None, 'shard')
- output_inner_grad: float32 [1536, 128], P('shard')
- output_outer_grad: float32 [128, 1536], P(None, 'shard')
- gate_inner_grad: float32 [1536, 128], P('shard')
- gate_outer_grad: float32 [128, 4096], P(None, 'shard')
- lift_inner_grad: float32 [1536, 128], P('shard')
- lift_outer_grad: float32 [128, 4096], P(None, 'shard')
- drop_inner_grad: float32 [4096, 128], P('shard')
- drop_outer_grad: float32 [128, 1536], P(None, 'shard')
All inputs are finite; a program needn't handle non-finite values.
Results may differ from a plain program's by a relative error of at most 0.02.
Values may be sent and summed in bfloat16 or wider, within the bound.
No kernel may reach another device: no remote copies, remote signals or barrier semaphores. Data moves between devices by JAX's collectives and lax.ppermute only.
A program may use at most 208 MiB of HBM per device.

v0:
```python
import functools
import math
from typing import NamedTuple

import jax
import jax.numpy as jnp
from jax import lax
from jax.experimental import pallas as pl
from jax.experimental.pallas import tpu as pltpu
from jax.sharding import PartitionSpec as P

HEADS = 16
KV_HEADS = 8
HEAD_DIM = 96
RANK = 16
ADAPTERS = 8
EPSILON = 1e-05
ROPE_BASE = 100000.0
MASKED_SCORE = -1e30
AXES = ("rep", "shard")
F32 = jnp.float32
BF16 = jnp.bfloat16


def move(value, target):
    reps, shards = lax.axis_size("rep"), lax.axis_size("shard")
    pairs = []
    for r in range(reps):
        for s in range(shards):
            r2, s2 = target(r, s)
            pairs.append((r * shards + s, r2 * shards + s2))
    return lax.ppermute(value, AXES, pairs)


def to_core(value):
    return move(value, lambda r, s: (r, s ^ 1))


def to_chip(value):
    return move(value, lambda r, s: (r, s ^ 2))


def to_y(value):
    return move(value, lambda r, s: (r ^ 1, s))


def to_z(value):
    return move(value, lambda r, s: (r ^ 2, s))


PANEL = 512
LANES = 128
PER_STEP = 2
EST = 5
PACK_EST = 0.1


class Piece(NamedTuple):
    parts: tuple
    row: int
    rows: int
    target: int
    block: int
    to_row: int
    to_col: int


class Bundle(NamedTuple):
    first: tuple
    second: tuple
    shapes: tuple
    joined: bool = True


def quarter_rows(pieces):
    return sum(p.rows for p in pieces) // 4


def make_bundles(width, kv_width, ff, chunks, shards):
    rows, drop_rows = width // shards, ff // shards // chunks
    panels = width // PANEL
    first = tuple(Piece(((0, c, PANEL),), 0, rows, 0, rows, 0, c) for c in range(0, width, PANEL))
    second = []
    for c in range(0, 2 * kv_width, PANEL):
        parts, at = [], c
        while at < c + PANEL:
            source = 1 if at < kv_width else 2
            base = (source - 1) * kv_width
            stop = min(c + PANEL, base + kv_width)
            parts.append((source, at - base, stop - at))
            at = stop
        second.append(Piece(tuple(parts), 0, rows, 0, rows, 0, width + c))
    found = [Bundle(first, tuple(second), ((width, width + 2 * kv_width),))]

    def halves(source, row, height, target, block):
        return [
            tuple(
                Piece(((source, i * PANEL, PANEL),), row + h * height // 2, height // 2, target, block,
                      h * height // 2, i * PANEL)
                for i in range(panels)
            )
            for h in range(2)
        ]

    top, bottom = halves(3, 0, rows, 0, rows)
    found.append(Bundle(top, bottom, ((width, width),)))
    part = ff // shards // chunks
    for u in range(chunks):
        sides = []
        for j in range(2):
            side = []
            for c in range(0, shards * part, PANEL):
                parts = tuple(
                    (4 + j, t * (ff // shards) + u * part, part)
                    for t in range(c // part, (c + PANEL) // part)
                )
                side.append(Piece(parts, 0, rows, 0, rows, 0, 2 * c + j * PANEL))
            sides.append(tuple(side))
        top, bottom = halves(6, u * drop_rows, drop_rows, 1, drop_rows)
        cols = shards * part
        found.append(
            Bundle(sides[0] + top, sides[1] + bottom, ((width, 2 * cols), (cols, width)), False)
        )
    return found


def work(microseconds):
    return pl.CostEstimate(flops=int(microseconds * 1.1e9), bytes_accessed=2**20, transcendentals=0)


def pack(place, jobs, operands, out_shapes, name):
    n_in, n_out = len(operands), len(out_shapes)

    def kernel(place_ref, *refs):
        ins, refs = refs[:n_in], refs[n_in:]
        outs, held, sems = refs[:n_out], refs[n_out : 2 * n_out], refs[-1]
        arriving, leaving = [], []
        for i, (src, o, *spot) in enumerate(jobs(place_ref, ins)):
            here = held[o].at[tuple(spot)]
            arriving.append(pltpu.make_async_copy(src, here, sems.at[0, i]))
            leaving.append(pltpu.make_async_copy(here, outs[o].at[tuple(spot)], sems.at[1, i]))
        for c in arriving:
            c.start()
        for c, d in zip(arriving, leaving):
            c.wait()
            d.start()
        for d in leaving:
            d.wait()

    class Fake:
        def __init__(self):
            self.at = self

        def __getitem__(self, _):
            return self

    count = len(jobs(None, [Fake()] * n_in))
    hbm = pl.BlockSpec(memory_space=pltpu.HBM)
    return pl.pallas_call(
        kernel,
        out_shape=[jax.ShapeDtypeStruct(sh, BF16) for sh in out_shapes],
        grid_spec=pltpu.PrefetchScalarGridSpec(
            num_scalar_prefetch=1,
            grid=(1,),
            in_specs=[hbm] * n_in,
            out_specs=[hbm] * n_out,
            scratch_shapes=[pltpu.VMEM(sh, BF16) for sh in out_shapes]
            + [pltpu.SemaphoreType.DMA((2, count))],
        ),
        compiler_params=pltpu.CompilerParams(vmem_limit_bytes=64 * 2**20),
        cost_estimate=work(PACK_EST),
        name=name,
    )(place, *operands)


def gate(value, ties):
    return pl.pallas_call(
        lambda *refs: None,
        out_shape=jax.ShapeDtypeStruct(value.shape, value.dtype),
        in_specs=[pl.BlockSpec(memory_space=pltpu.HBM)] * (1 + len(ties)),
        out_specs=pl.BlockSpec(memory_space=pltpu.HBM),
        input_output_aliases={0: 0},
        compiler_params=pltpu.CompilerParams(vmem_limit_bytes=64 * 2**20),
        name="gate",
    )(value, *ties)


def join(*parts, ties=()):
    cols = parts[0].shape[1]

    def kernel(*refs):
        at = 0
        for ref in refs[: len(parts)]:
            refs[-1][at : at + ref.shape[0]] = ref[...]
            at += ref.shape[0]

    return pl.pallas_call(
        kernel,
        out_shape=jax.ShapeDtypeStruct((sum(p.shape[0] for p in parts), cols), parts[0].dtype),
        in_specs=[pl.BlockSpec(memory_space=pltpu.VMEM)] * len(parts)
        + [pl.BlockSpec(memory_space=pltpu.HBM)] * len(ties),
        compiler_params=pltpu.CompilerParams(vmem_limit_bytes=64 * 2**20),
        cost_estimate=work(1),
        name="join",
    )(*parts, *ties)


def quarter_start(place_ref, flip, rows):
    if place_ref is None:
        return 0
    return pl.multiple_of((place_ref[1] ^ flip) * rows, 16)


class Relay:
    def __init__(self, place, weights, bundles):
        self.place, self.weights, self.bundles = place, weights, bundles
        self.direct, self.once, self.twice = {}, {}, {}
        self.here, self.there = {}, {}
        self.tick = 0

    def step(self, extra=(), ties=(), across=True):
        t, bundles = self.tick, self.bundles
        self.tick += 1
        operands, shapes, kinds, sent = [], [], [], []

        def operand(array):
            for i, o in enumerate(operands):
                if o is array:
                    return i
            operands.append(array)
            return len(operands) - 1

        plans = []

        def out(kind, rows, cols=PANEL):
            shapes.append((rows, cols))
            kinds.append(kind)
            return len(shapes) - 1

        if t < len(bundles):
            b = bundles[t]
            base = quarter_rows(b.first + b.second)
            o = out("x", base + sum(n * a.shape[2] // PANEL for a, _, n in extra))
            for array, start, count in extra:
                i = operand(array)
                sent.append((base, count))

                def plan_t(pr, ins, o=o, i=i, start=start, count=count, base=base, cols=array.shape[2]):
                    which = 0 if pr is None else 1 - pr[0] // 2
                    return [
                        (ins[i].at[which, pl.ds(start, count), pl.ds(c, PANEL)], o,
                         pl.ds(base + c // PANEL * count, count), slice(None))
                        for c in range(0, cols, PANEL)
                    ]

                plans.append(plan_t)
                base += count * array.shape[2] // PANEL
            used = [(operand(self.weights[q[0]]), q, p) for p in b.first + b.second for q in p.parts]

            def plan_x(pr, ins, o=o, used=used):
                copies, at, col = [], 0, 0
                for i, (_, c, n), p in used:
                    q = p.rows // 4
                    rows = pl.ds(pl.multiple_of(p.row + quarter_start(pr, 0, q), 16), q)
                    copies.append((ins[i].at[rows, pl.ds(c, n)],
                                   o, pl.ds(at, q), pl.ds(col, n)))
                    col += n
                    if col == PANEL:
                        at, col = at + q, 0
                return copies

            plans.append(plan_x)
        y_parts, z_parts = [], []
        b1, b2, b3 = t - 1, t - 2, t - 3
        if 0 <= b1 < len(bundles):
            qa, qb = quarter_rows(bundles[b1].first), quarter_rows(bundles[b1].second)
            y_parts.append(("first", b1, [(self.direct[b1], 0, qa)]))
            z_parts.append(("first", b1, [(self.direct[b1], qa, qb)]))
        if 0 <= b2 < len(bundles):
            qa, qb = quarter_rows(bundles[b2].first), quarter_rows(bundles[b2].second)
            (ya, yo), (za, zo) = self.once[b2]
            y_parts.append(("second", b2, [(self.direct[b2], qa, qb), (za, zo, qb)]))
            z_parts.append(("second", b2, [(self.direct[b2], 0, qa), (ya, yo, qa)]))
        for kind, parts in (("y", y_parts), ("z", z_parts)):
            if not parts:
                continue
            total = sum(n for _, _, l in parts for _, _, n in l)
            o = out(kind, total)
            flat = [(operand(a), r, n) for _, _, l in parts for a, r, n in l]

            def plan_n(pr, ins, o=o, flat=flat):
                copies, at = [], 0
                for i, r, n in flat:
                    copies.append((ins[i].at[pl.ds(r, n)], o, pl.ds(at, n), slice(None)))
                    at += n
                return copies

            plans.append(plan_n)
        for tie in ties:
            operand(tie)

        def jobs(pr, ins):
            return [c for plan in plans for c in plan(pr, ins)]

        bufs = pack(self.place, jobs, operands, shapes, f"pack_{t}") if shapes else []
        for kind, buf in zip(kinds, bufs):
            if kind == "x":
                self.direct[t] = to_chip(buf)
            else:
                got = (to_y if kind == "y" else to_z)(buf)
                at = 0
                for stage, bi, l in y_parts if kind == "y" else z_parts:
                    store = self.once if stage == "first" else self.twice
                    pair = store.setdefault(bi, [None, None])
                    pair[0 if kind == "y" else 1] = (got, at)
                    at += sum(n for _, _, n in l)
        if 0 <= b3 < len(bundles) and across:
            self.across(b3, bufs[:1] if bufs else ties)
        return [(self.direct[t], *spot) for spot in sent], bufs

    def across(self, b3, ties):
        b = self.bundles[b3]
        operands, shapes = [], []

        def operand(array):
            for i, o in enumerate(operands):
                if o is array:
                    return i
            operands.append(array)
            return len(operands) - 1

        plans = []

        def out(kind, rows, cols=PANEL):
            shapes.append((rows, cols))
            return len(shapes) - 1

        total = 4 * quarter_rows(b.first + b.second)
        o = out("c", (2 if b.joined else 1) * total)
        used = [
            (operand(self.weights[q[0]]), q, p)
            for p in (b.first + b.second if b.joined else ()) for q in p.parts
        ]
        qa = quarter_rows(b.first)
        qb = quarter_rows(b.second)
        (ya, yo), (za, zo) = self.once[b3]
        (ys, yso), (zs, zso) = self.twice[b3]
        d = operand(self.direct[b3])
        sides = [
            (b.first, [(0, d, 0), (1, operand(ya), yo), (2, operand(zs), zso), (3, operand(zs), zso + qa)]),
            (b.second, [(0, d, qa), (2, operand(za), zo), (1, operand(ys), yso), (3, operand(ys), yso + qb)]),
        ]

        def plan_c(pr, ins, o=o, sides=sides, used=used, total=total):
            copies, base, at, col = [], total if b.joined else 0, 0, 0
            for i, (_, c, n), p in used:
                copies.append((ins[i].at[pl.ds(p.row, p.rows), pl.ds(c, n)],
                               o, pl.ds(at, p.rows), pl.ds(col, n)))
                col += n
                if col == PANEL:
                    at, col = at + p.rows, 0
            for pieces, quarters in sides:
                at = 0
                for p in pieces:
                    q = p.rows // 4
                    for flip, i, r in quarters:
                        to = pl.multiple_of(base + quarter_start(pr, flip, q), 16)
                        copies.append((ins[i].at[pl.ds(r + at, q)], o, pl.ds(to, q), slice(None)))
                    at += q
                    base += p.rows
            return copies

        plans.append(plan_c)

        for tie in ties:
            operand(tie)
        jobs = lambda pr, ins: plans[0](pr, ins)
        (buf,) = pack(self.place, jobs, operands, shapes, f"across_{b3}")
        self.here[b3], self.there[b3] = buf, to_core(buf)


def land_copies(place_ref, bundle, own, near, here, there, targets):
    copies = []
    shard = 0 if place_ref is None else place_ref[0]
    pieces = bundle.first + bundle.second
    total = sum(p.rows for p in pieces)
    skip = total if bundle.joined else 0
    for slot, (ref, base) in enumerate(((None, 0), (there, 0), (here, skip), (there, skip))):
        for p in pieces:
            to = (shard ^ slot) * p.block + p.to_row
            to = pl.ds(pl.multiple_of(to, 16), p.rows)
            dst = targets[p.target]
            key = (p.target, p.to_col)
            if slot == 0 or slot == 1 and not bundle.joined:
                col = p.to_col
                for source, c, n in p.parts:
                    copies.append(((near if slot else own)[source].at[pl.ds(p.row, p.rows), pl.ds(c, n)],
                                   dst.at[to, pl.ds(col, n)], key))
                    col += n
            else:
                copies.append((ref.at[pl.ds(base, p.rows)], dst.at[to, pl.ds(p.to_col, PANEL)], key))
            base += p.rows
    return copies


def sources_of(bundle):
    return sorted({q[0] for p in bundle.first + bundle.second for q in p.parts})


def rotary_tables(positions, head_dim):
    half_dim = head_dim // 2
    freq_index = jnp.arange(half_dim).astype(F32)
    frequency = jnp.exp(freq_index * (-2.0 * math.log(ROPE_BASE) / head_dim))
    angles = positions[:, None] * frequency[None, :]
    return jnp.cos(angles), jnp.sin(angles)


def dot(left, right):
    return jnp.dot(left, right, preferred_element_type=F32)


def dot_nt(left, right):
    return lax.dot_general(left, right, (((1,), (1,)), ((), ())), preferred_element_type=F32)


def dot_tn(left, right):
    return lax.dot_general(left, right, (((0,), (0,)), ((), ())), preferred_element_type=F32)


LOG2E = 1.4426950408889634


def last_visible(place_ref, low, lanes, block):
    shard, prefix = place_ref[0], place_ref[2]
    at = shard % 2 if low else 2 + shard % 2
    position = at * block + lax.broadcasted_iota(jnp.int32, (1, lanes), 1) % block
    return jnp.maximum(position + 1, prefix)


def query_start(place_ref, low, block):
    chip = place_ref[0] // 2
    return pl.multiple_of((chip if low else 1 - chip) * block, block)


def natural_rows(place_ref, own, near, into, block, n):
    shard = place_ref[0]
    for slot, value in (
        (0, own[n, :block]),
        (2, own[n, block:]),
        (1, near[n, :block]),
        (3, near[n, block:]),
    ):
        into[n, pl.ds(pl.multiple_of((shard ^ slot) * block, block), block)] = value


def hide(scores, limit, first_key):
    keys = first_key + lax.broadcasted_iota(jnp.int32, scores.shape, 0)
    return jnp.where(keys < limit, scores, MASKED_SCORE)


def masked_by_part(low, scores, limit, block):
    if low:
        return hide(scores, limit, 0)
    half = 2 * block
    return jnp.concatenate([scores[:half], hide(scores[half:], limit, half)], axis=0)


def attend_kernel(place, q, k_own, k_near, v_own, v_near, out, lse, keys, values, *, scale):
    block = q.shape[1] // 2
    count_kv = k_own.shape[0]
    group = q.shape[0] // count_kv
    for n in range(count_kv):
        natural_rows(place, k_own, k_near, keys, block, n)
        natural_rows(place, v_own, v_near, values, block, n)
    for n in range(count_kv):
        values_t = values[n].T
        for part, low in enumerate((True, False)):
            count = (2 if low else 4) * block
            rows = pl.ds(query_start(place, low, block), block)
            query = jnp.concatenate([q[n * group + j, rows] for j in range(group)], axis=0)
            limit = last_visible(place, low, group * block, block)
            scores = masked_by_part(low, dot_nt(keys[n, :count], query), limit, block)
            top = jnp.max(scores, axis=0, keepdims=True)
            base = scale * LOG2E
            expo = jnp.exp2(scores * base - top * base)
            total = jnp.sum(expo, axis=0, keepdims=True)
            lse[n, part] = (top * base + jnp.log2(total))[0]
            result = dot(values_t[:, :count], expo.astype(BF16)) / total
            result = result.T.astype(BF16)
            for j in range(group):
                out[n * group + j, rows] = result[j * block : (j + 1) * block]


def attend(place, queries, kv_own, kv_near):
    heads, rows, dim = queries.shape
    kv_heads = kv_own.shape[0] // 2
    group = heads // kv_heads
    per = PER_STEP
    q_spec = pl.BlockSpec((per * group, rows, dim), lambda g, p: (g, 0, 0))
    kv_spec = pl.BlockSpec((per, rows, dim), lambda g, p: (g, 0, 0))
    v_spec = pl.BlockSpec((per, rows, dim), lambda g, p: (g + kv_heads // per, 0, 0))
    lse_shape = (kv_heads, 2, group * rows // 2)
    return pl.pallas_call(
        functools.partial(attend_kernel, scale=HEAD_DIM ** (-0.5)),
        out_shape=[
            jax.ShapeDtypeStruct(queries.shape, BF16),
            jax.ShapeDtypeStruct(lse_shape, F32),
        ],
        grid_spec=pltpu.PrefetchScalarGridSpec(
            num_scalar_prefetch=1,
            grid=(kv_heads // per,),
            in_specs=[q_spec, kv_spec, kv_spec, v_spec, v_spec],
            out_specs=[q_spec, pl.BlockSpec((per, *lse_shape[1:]), lambda g, p: (g, 0, 0))],
            scratch_shapes=[pltpu.VMEM((per, 2 * rows, dim), BF16)] * 2,
        ),
        compiler_params=pltpu.CompilerParams(vmem_limit_bytes=64 * 2**20),
        cost_estimate=work(EST),
        name="attend",
    )(place, queries, kv_own, kv_near, kv_own, kv_near)


def attend_back_kernel(
    place, q, k_own, k_near, v_own, v_near, grad, lse, cos_t, sin_t, *rest, scale
):
    dq, own_out, send_out, keys, values, dk, dv = rest[-7:]
    block = q.shape[1] // 2
    count_kv = k_own.shape[0]
    group = q.shape[0] // count_kv
    half = HEAD_DIM // 2
    for n in range(count_kv):
        natural_rows(place, k_own, k_near, keys, block, n)
        natural_rows(place, v_own, v_near, values, block, n)
    for n in range(count_kv):
        keys_t = keys[n].T
        for part, low in ((1, False), (0, True)):
            count = (2 if low else 4) * block
            start = query_start(place, low, block)
            rows = pl.ds(start, block)
            query = jnp.concatenate([q[n * group + j, rows] for j in range(group)], axis=0)
            out_grad = jnp.concatenate([grad[n * group + j, rows] for j in range(group)], axis=0)
            limit = last_visible(place, low, group * block, block)
            scores = masked_by_part(low, dot_nt(keys[n, :count], query), limit, block)
            probs = jnp.exp2(scores * (scale * LOG2E) - lse[n, part][None])
            probs_grad = dot_nt(values[n, :count], out_grad)
            mean = jnp.sum(probs * probs_grad, axis=0, keepdims=True)
            score_grad = (probs * (probs_grad - mean)).astype(BF16)
            v_part = dot(probs.astype(BF16), out_grad)
            k_part = dot(score_grad, query) * scale
            if low:
                dk[n, :count] += k_part
                dv[n, :count] += v_part
            else:
                dk[n] = k_part
                dv[n] = v_part
            turned = dot(keys_t[:, :count], score_grad) * scale
            cos = jnp.concatenate([cos_t[:, rows]] * group, axis=1)
            sin = jnp.concatenate([sin_t[:, rows]] * group, axis=1)
            u, w = turned[:half], turned[half : 2 * half]
            pad = jnp.zeros((q.shape[2] - 2 * half, u.shape[1]), F32)
            turned = jnp.concatenate([u * cos + w * sin, w * cos - u * sin, pad], axis=0)
            turned = turned.T.astype(BF16)
            for j in range(group):
                dq[n * group + j, rows] = turned[j * block : (j + 1) * block]
        shard = place[0]
        for slot, at, own in ((0, 0, True), (2, 1, True), (1, 0, False), (3, 1, False)):
            rows = pl.ds(pl.multiple_of((shard ^ slot) * block, block), block)
            to = slice(at * block, (at + 1) * block)
            out = own_out if own else send_out
            out[0, n, to] = dk[n, rows].astype(out.dtype)
            out[1, n, to] = dv[n, rows].astype(out.dtype)


def attend_back(place, queries, kv_own, kv_near, grad, lse, cos_t, sin_t, part, parts, ties):
    heads, rows, dim = queries.shape
    kv_heads = kv_own.shape[0] // 2
    group = heads // kv_heads
    count = kv_heads // parts
    per = PER_STEP
    base = part * count // per
    q_spec = pl.BlockSpec((per * group, rows, dim), lambda g, p: (g + base, 0, 0))
    kv_spec = pl.BlockSpec((per, rows, dim), lambda g, p: (g + base, 0, 0))
    v_spec = pl.BlockSpec((per, rows, dim), lambda g, p: (g + base + kv_heads // per, 0, 0))
    whole = pl.BlockSpec(cos_t.shape, lambda g, p: (0, 0))
    return pl.pallas_call(
        functools.partial(attend_back_kernel, scale=HEAD_DIM ** (-0.5)),
        out_shape=[
            jax.ShapeDtypeStruct((heads // parts, rows, dim), BF16),
            jax.ShapeDtypeStruct((2, count, rows, dim), F32),
            jax.ShapeDtypeStruct((2, count, rows, dim), BF16),
        ],
        grid_spec=pltpu.PrefetchScalarGridSpec(
            num_scalar_prefetch=1,
            grid=(count // per,),
            in_specs=[q_spec, kv_spec, kv_spec, v_spec, v_spec]
            + [q_spec, pl.BlockSpec((per, *lse.shape[1:]), lambda g, p: (g + base, 0, 0)), whole, whole]
            + [pl.BlockSpec(memory_space=pltpu.HBM)] * len(ties),
            out_specs=[pl.BlockSpec((per * group, rows, dim), lambda g, p: (g, 0, 0))] + [pl.BlockSpec((2, per, rows, dim), lambda g, p: (0, g, 0, 0))] * 2,
            scratch_shapes=[pltpu.VMEM((per, 2 * rows, dim), BF16)] * 2
            + [pltpu.VMEM((per, 2 * rows, dim), F32)] * 2,
        ),
        compiler_params=pltpu.CompilerParams(vmem_limit_bytes=64 * 2**20),
        cost_estimate=work(1),
        name=f"attend_back_{part}",
    )(place, queries, kv_own, kv_near, kv_own, kv_near, grad, lse, cos_t, sin_t, *ties)


def row_copies(sources, refs, into, sems):
    copies, at = [], into.shape[0] // 2
    for ref, (_, base, count) in zip(refs, sources):
        for c in range(into.shape[1] // PANEL):
            copies.append(
                pltpu.make_async_copy(
                    ref.at[pl.ds(base + c * count, count)],
                    into.at[pl.ds(at, count), pl.ds(c * PANEL, PANEL)],
                    sems.at[len(copies)],
                )
            )
        at += count
    return copies


class Landing:
    def __init__(self, place, bundle, refs, targets, sems):
        used = sources_of(bundle)
        n = len(used)
        own = dict(zip(used, refs[:n]))
        near = {} if bundle.joined else dict(zip(used, refs[n : 2 * n]))
        listed = land_copies(place, bundle, own, near, refs[-2], refs[-1], targets)
        self.copies = [
            (key, pltpu.make_async_copy(src, dst, sems.at[i])) for i, (src, dst, key) in enumerate(listed)
        ]
        self.copies.sort(key=lambda c: c[0])
        for _, c in self.copies:
            c.start()

    def wait(self, wanted=None):
        left = []
        for key, c in self.copies:
            if wanted is None or wanted(key):
                c.wait()
            else:
                left.append((key, c))
        self.copies = left


def landing_operands(bundle, weights, near, here, there):
    used = sources_of(bundle)
    return [weights[i] for i in used] + ([] if bundle.joined else [near[i] for i in used]) + [here, there]


def landing_count(bundle):
    return sum((1 if bundle.joined else 2) * len(p.parts) + 3 for p in bundle.first + bundle.second)


NO_BUNDLE = Bundle((), (), ())


def kernel_call(body, place, bundle, landing, operands, outs, scratch, name, time=0.5, ties=()):
    operands = [*operands, *((t, HB) for t in ties)]
    n_land, n_in, n_out, n_w = len(landing), len(operands), len(outs), len(bundle.shapes)

    def kernel(place_ref, *refs):
        land, refs = refs[:n_land], refs[n_land:]
        ins, refs = refs[: n_in - len(ties)], refs[n_in:]
        out, refs = refs[:n_out], refs[n_out:]
        body(place_ref, land, ins, out, refs[:n_w], refs[n_w], refs[n_w + 1 :])

    def spec(where):
        return where if isinstance(where, pl.BlockSpec) else pl.BlockSpec(memory_space=where)

    return pl.pallas_call(
        kernel,
        out_shape=[o for o, _ in outs],
        grid_spec=pltpu.PrefetchScalarGridSpec(
            num_scalar_prefetch=1,
            grid=(1,),
            in_specs=[spec(pltpu.HBM)] * n_land + [spec(w) for _, w in operands],
            out_specs=[spec(w) for _, w in outs],
            scratch_shapes=[pltpu.VMEM(sh, BF16) for sh in bundle.shapes]
            + [pltpu.SemaphoreType.DMA((max(landing_count(bundle), 1),))]
            + list(scratch),
        ),
        compiler_params=pltpu.CompilerParams(vmem_limit_bytes=64 * 2**20),
        cost_estimate=work(time),
        name=name,
    )(place, *landing, *[a for a, _ in operands])


VM = pltpu.VMEM
HB = pltpu.HBM


def like(shape, dtype):
    return jax.ShapeDtypeStruct(shape, dtype)


def turn(value, cos_full, sin_signed, half):
    swapped = jnp.concatenate([value[:, half:], value[:, :half]], axis=1)
    return value * cos_full + swapped * sin_signed


def padded(value):
    return jnp.concatenate([value, jnp.zeros((value.shape[0], LANES - HEAD_DIM), value.dtype)], axis=1)


def one_of_pair(block, width):
    return pl.BlockSpec((None, block, width), lambda i, p: (p[0] // 2, 0, 0))


def qkv_forward(place, bundle, landing, tokens, tokens_back, gain, inner, outer, cos, sin, ties):
    _, block, width = tokens.shape
    rows = 2 * block
    total = bundle.shapes[0][1]
    kv = (total - width) // 2
    wide = 8 * HEAD_DIM
    half = HEAD_DIM // 2

    def body(pr, land_refs, ins, outs, weights, sems, scratch):
        kept, *backs, gain_ref, inner_ref, outer_ref, cos_ref, sin_ref = ins
        q, kv_ref, hidden_ref, normed_ref, x_ref = outs
        (w,) = weights
        arriving = row_copies(tokens_back, backs, x_ref, scratch[0])
        for c in arriving:
            c.start()
        landing = Landing(pr, bundle, land_refs, weights, sems)
        x_ref[:block] = kept[...]
        for c in arriving:
            c.wait()
        x = x_ref[...].astype(F32)
        scale = lax.rsqrt(jnp.mean(x * x, axis=-1, keepdims=True) + EPSILON)
        normed_ref[...] = (x * scale * gain_ref[...].astype(F32)).astype(BF16)
        hidden_ref[...] = dot_nt(normed_ref[...], inner_ref[...]).astype(BF16)

        def columns(at):
            cols = pl.ds(at, wide)
            return dot(normed_ref[...], w[:, cols]) + dot(hidden_ref[...], outer_ref[:, cols])

        landing.wait(lambda key: key[1] < width)
        for i in range(width // wide):
            acc = columns(i * wide)
            for h in range(8):
                one = acc[:, h * HEAD_DIM : (h + 1) * HEAD_DIM]
                q[8 * i + h] = padded(turn(one, cos_ref[...], sin_ref[...], half)).astype(BF16)
        landing.wait()
        acc = columns(width)
        for h in range(8):
            one = acc[:, h * HEAD_DIM : (h + 1) * HEAD_DIM]
            kv_ref[h] = padded(turn(one, cos_ref[...], sin_ref[...], half)).astype(BF16)
        acc = columns(width + kv)
        for h in range(8):
            kv_ref[8 + h] = padded(acc[:, h * HEAD_DIM : (h + 1) * HEAD_DIM]).astype(BF16)

    heads = width // HEAD_DIM
    return kernel_call(
        body, place, bundle, landing,
        [(tokens, one_of_pair(block, width)), *((t[0], HB) for t in tokens_back), (gain, VM), (inner, VM), (outer, VM), (cos, VM), (sin, VM)],
        [
            (like((heads, rows, LANES), BF16), VM),
            (like((2 * kv // HEAD_DIM, rows, LANES), BF16), VM),
            (like((rows, inner.shape[0]), BF16), VM),
            (like((rows, width), BF16), VM),
            (like((rows, width), BF16), VM),
        ],
        [pltpu.SemaphoreType.DMA((len(tokens_back) * width // PANEL,))], "qkv_forward", time=EST, ties=ties,
    )


def out_forward(place, bundle, landing, heads_out, x, gain, inner, outer, cot, cot_back, inner_gl, drop_b):
    rows, width = x.shape
    heads = heads_out.shape[0]

    def body(pr, land_refs, ins, outs, weights, sems, scratch):
        heads_ref, x_ref, gain_ref, inner_ref, outer_ref, cot_kept, *cot_got, igl, db = ins
        middle, normed, attended, hidden, cot_ref, h_gl, h_d = outs
        arriving = row_copies(cot_back, cot_got, cot_ref, scratch[0])
        for c in arriving:
            c.start()
        landing = Landing(pr, bundle, land_refs, weights, sems)
        for h in range(heads):
            attended[:, h * HEAD_DIM : (h + 1) * HEAD_DIM] = heads_ref[h, :, :HEAD_DIM]
        hidden[...] = dot_nt(attended[...], inner_ref[...]).astype(BF16)
        cot_ref[: rows // 2] = cot_kept[...]
        for c in arriving:
            c.wait()
        h_d[...] = dot_nt(cot_ref[...], db[...]).astype(BF16)
        landing.wait()
        wide = width // 2
        squares = jnp.zeros((rows, 1), F32)
        for i in range(2):
            cols = pl.ds(i * wide, wide)
            branch = dot(attended[...], weights[0][:, cols]) + dot(hidden[...], outer_ref[:, cols])
            value = x_ref[:, cols].astype(F32) + branch
            middle[:, cols] = value
            squares += jnp.sum(value * value, axis=-1, keepdims=True)
        scale = lax.rsqrt(squares / width + EPSILON)
        normed[...] = (middle[...] * scale * gain_ref[...].astype(F32)).astype(BF16)
        h_gl[...] = dot_nt(normed[...], igl[...]).astype(BF16)

    return kernel_call(
        body, place, bundle, landing,
        [(heads_out, VM), (x, VM), (gain, VM), (inner, VM), (outer, VM),
         (cot, one_of_pair(rows // 2, width)), *((c[0], HB) for c in cot_back), (inner_gl, VM), (drop_b, VM)],
        [
            (like((rows, width), F32), VM),
            (like((rows, width), BF16), VM),
            (like((rows, width), BF16), VM),
            (like((rows, RANK), BF16), VM),
            (like((rows, width), BF16), VM),
            (like((rows, 2 * RANK), BF16), VM),
            (like((rows, RANK), BF16), VM),
        ],
        [pltpu.SemaphoreType.DMA((len(cot_back) * width // PANEL,))], "out_forward", time=EST,
    )


def mlp_chunk(place, bundle, landing, normed, cot, hidden_gl, hidden_d, outer_gl, drop_a, chunk, sums, name):
    rows, width = normed.shape
    units = bundle.shapes[1][0]
    steps = units // PANEL
    first = sums is None
    part = units // 4

    def body(pr, land_refs, ins, outs, weights, sems, scratch):
        normed_ref, cot_ref, hgl_ref, hd_ref, ogl, da = ins[:6]
        drop_sum, e_sum, thin, keep, send = outs
        (packed,) = scratch
        w_gl, w_d = weights
        landing = Landing(pr, bundle, land_refs, weights, sems)
        h_d = hd_ref[...]
        h_g, h_l = hgl_ref[:, :RANK], hgl_ref[:, RANK:]
        g_t, l_t, d_t = h_g.T, h_l.T, h_d.T
        for i in range(steps):
            landing.wait(lambda key: key[0] == 1 or key[1] < 2 * (i + 1) * PANEL)
            cols = slice(i * PANEL, (i + 1) * PANEL)
            both = pl.ds(2 * i * PANEL, 2 * PANEL)
            acts = dot(normed_ref[...], w_gl[:, both])
            gate = acts[:, :PANEL] + dot(h_g, ogl[:RANK, cols])
            lift = acts[:, PANEL:] + dot(h_l, ogl[RANK:, cols])
            a_grad = dot_nt(cot_ref[...], w_d[cols]) + dot(h_d, da[:, cols])
            sig = 1.0 / (1.0 + jnp.exp(-gate))
            silu = gate * sig
            active = (silu * lift).astype(BF16)
            gate_grad = (a_grad * lift * sig * (1.0 + gate * (1.0 - sig))).astype(BF16)
            lift_grad = (a_grad * silu).astype(BF16)
            grads = jnp.concatenate([gate_grad, lift_grad], axis=1)
            down = dot(active, w_d[cols])
            back = dot_nt(grads, w_gl[:, both])
            t0 = dot_nt(active, da[:, cols])
            t1 = dot_nt(gate_grad, ogl[:RANK, cols])
            t2 = dot_nt(lift_grad, ogl[RANK:, cols])
            if i == 0 and first:
                drop_sum[...] = down
                e_sum[...] = back
                thin[0], thin[1], thin[2] = t0, t1, t2
            elif i == 0:
                drop_sum[...] = ins[6][...] + down
                e_sum[...] = ins[7][...] + back
                thin[0], thin[1], thin[2] = ins[8][0] + t0, ins[8][1] + t1, ins[8][2] + t2
            else:
                drop_sum[...] += down
                e_sum[...] += back
                thin[0] += t0
                thin[1] += t1
                thin[2] += t2
            per = PANEL // part
            for j, g in enumerate((dot(g_t, gate_grad), dot(l_t, lift_grad), dot(d_t, active))):
                for o in range(per):
                    packed[i * per + o, :, j * part : (j + 1) * part] = g[:, o * part : (o + 1) * part]
        split_by_core(pr, packed, keep, send)

    at_chunk = lambda i, p: (chunk, 0, 0)
    operands = [
        (normed, VM), (cot, VM), (hidden_gl, VM), (hidden_d, VM),
        (outer_gl, pl.BlockSpec((None, *outer_gl.shape[1:]), at_chunk)),
        (drop_a, pl.BlockSpec((None, *drop_a.shape[1:]), at_chunk)),
    ]
    if not first:
        operands += [(s, VM) for s in sums]
    return kernel_call(
        body, place, bundle, landing, operands,
        [
            (like((rows, width), F32), VM),
            (like((rows, width), F32), VM),
            (like((3, rows, RANK), F32), VM),
            (like((2, RANK, 3 * part), F32), VM),
            (like((2, RANK, 3 * part), BF16), VM),
        ],
        [pltpu.VMEM((4, RANK, 3 * part), F32)], name, time=EST,
    )


def split_by_core(place_ref, whole, keep, send):
    core = place_ref[0] % 2
    for j in range(2):
        keep[j] = whole[core + 2 * j]
        send[j] = whole[1 - core + 2 * j].astype(BF16)


def out_backward(place, bundle, landing, sums, middle, cot, gain, normed, attended, hidden, factors, ties):
    rows, width = middle.shape
    heads = width // HEAD_DIM

    def body(pr, land_refs, ins, outs, weights, sems, scratch):
        drop_sum, e_sum, thin, middle_ref, cot_ref, gain_ref, normed_ref, att, hid, drop_b, igl, o_a, o_b = ins
        mixed_kept, mixed_back, mid_grad, out_heads, keep, send = outs
        (w,) = weights
        branch, whole = scratch
        landing = Landing(pr, bundle, land_refs, weights, sems)
        d_hid = thin[0].astype(BF16)
        gl_grad = jnp.concatenate([thin[1].astype(BF16), thin[2].astype(BF16)], axis=1)
        e_in = (e_sum[...] + dot(gl_grad, igl[...])) * gain_ref[...].astype(F32)
        mid = middle_ref[...]
        scale = lax.rsqrt(jnp.mean(mid * mid, axis=-1, keepdims=True) + EPSILON)
        n = mid * scale
        mean = jnp.mean(e_in * n, axis=-1, keepdims=True)
        mid_grad[...] = cot_ref[...].astype(F32) + scale * (e_in - n * mean)
        branch[...] = mid_grad[...].astype(BF16)
        hgrad = dot_nt(branch[...], o_b[...]).astype(BF16)
        landing.wait()
        wide = 8 * HEAD_DIM
        for i in range(heads // 8):
            part = slice(i * wide, (i + 1) * wide)
            grad = dot_nt(branch[...], w[part]) + dot(hgrad, o_a[:, part])
            for h in range(8):
                out_heads[8 * i + h] = padded(grad[:, h * HEAD_DIM : (h + 1) * HEAD_DIM]).astype(BF16)
        mixed = (mid + drop_sum[...] + dot(d_hid, drop_b[...])).astype(BF16)
        mixed_kept[...] = mixed[: rows // 2]
        mixed_back[...] = mixed[rows // 2 :]
        gl = dot(gl_grad.T, normed_ref[...])
        own = (
            dot(d_hid.T, cot_ref[...]), gl[:RANK], gl[RANK:],
            dot(hgrad.T, att[...]), dot(hid[...].T, branch[...]),
        )
        for t in range(4):
            for j, g in enumerate(own):
                at = j * quarter
                whole[t, :, at : at + quarter] = g[:, t * quarter : (t + 1) * quarter]
        split_by_core(pr, whole, keep, send)

    quarter = width // 4
    cols = 5 * quarter
    return kernel_call(
        body, place, bundle, landing,
        [(v, VM) for v in (*sums, middle, cot, gain, normed, attended, hidden, *factors)],
        [
            (like((2, rows // 2, width), BF16), one_of_pair(rows // 2, width)),
            (like((rows // 2, width), BF16), VM),
            (like((rows, width), F32), VM),
            (like((heads, rows, LANES), BF16), VM),
            (like((2, RANK, cols), F32), VM),
            (like((2, RANK, cols), BF16), VM),
        ],
        [pltpu.VMEM((rows, width), BF16), pltpu.VMEM((4, RANK, cols), F32)], "out_backward", time=15, ties=ties,
    )


def qkv_gradients(place, parts, cos, sin, normed, hidden, outer, ties):
    rows, width = normed.shape
    total = outer.shape[1]
    kv = (total - width) // 2
    half = HEAD_DIM // 2
    rank3 = outer.shape[0]
    quarter, kv_quarter = width // 4, kv // 4
    cols = 4 * quarter + 2 * kv_quarter
    q_count, kv_count = parts[0][0].shape[0], parts[0][1].shape[1]

    def body(pr, land_refs, ins, outs, weights, sems, scratch):
        *part_refs, cos_ref, sin_ref, nrm, hid, b = ins
        dq_refs, dkv_refs, got_refs = part_refs[0::3], part_refs[1::3], part_refs[2::3]
        g, hgrad_ref, keep, send = outs
        (whole,) = scratch
        for h in range(width // HEAD_DIM):
            ref, i = dq_refs[h // q_count], h % q_count
            g[:, h * HEAD_DIM : (h + 1) * HEAD_DIM] = ref[i, :, :HEAD_DIM]
        for h in range(kv // HEAD_DIM):
            dkv_ref, got_ref, i = dkv_refs[h // kv_count], got_refs[h // kv_count], h % kv_count
            one = (dkv_ref[0, i] + got_ref[0, i].astype(F32))[:, :HEAD_DIM]
            at = width + h * HEAD_DIM
            g[:, at : at + HEAD_DIM] = turn(one, cos_ref[...], -sin_ref[...], half).astype(BF16)
            at += kv
            g[:, at : at + HEAD_DIM] = (dkv_ref[1, i] + got_ref[1, i].astype(F32))[:, :HEAD_DIM].astype(BF16)
        hgrad_ref[...] = dot_nt(g[...], b[...]).astype(BF16)
        g_in = dot(hgrad_ref[...].T, nrm[...])
        g_out = dot(hid[...].T, g[...])
        for t in range(4):
            for i in range(3):
                whole[t, :, i * quarter : (i + 1) * quarter] = g_in[
                    i * RANK : (i + 1) * RANK, t * quarter : (t + 1) * quarter
                ]
            whole[t, :, 3 * quarter : 4 * quarter] = g_out[:RANK, t * quarter : (t + 1) * quarter]
            for i in range(2):
                at, start = 4 * quarter + i * kv_quarter, width + i * kv + t * kv_quarter
                whole[t, :, at : at + kv_quarter] = g_out[
                    (1 + i) * RANK : (2 + i) * RANK, start : start + kv_quarter
                ]
        split_by_core(pr, whole, keep, send)

    return kernel_call(
        body, place, NO_BUNDLE, [],
        [(v, VM) for v in (*[v for p in parts for v in p], cos, sin, normed, hidden, outer)],
        [
            (like((rows, total), BF16), VM),
            (like((rows, rank3), BF16), VM),
            (like((2, RANK, cols), F32), VM),
            (like((2, RANK, cols), BF16), VM),
        ],
        [pltpu.VMEM((4, RANK, cols), F32)], "qkv_gradients", time=1, ties=ties,
    )


def qkv_backward(place, bundle, landing, g, hgrad, x, mid_grad, gain, inner, ties):
    rows, width = x.shape
    total = bundle.shapes[0][1]
    block = rows // 2

    def body(pr, land_refs, ins, outs, weights, sems, scratch):
        g_ref, hg, x_ref, mg, gain_ref, a = ins
        kept, back = outs
        (w,) = weights
        landing = Landing(pr, bundle, land_refs, weights, sems)
        xf = x_ref[...].astype(F32)
        scale = lax.rsqrt(jnp.mean(xf * xf, axis=-1, keepdims=True) + EPSILON)
        n = xf * scale
        thin = dot(hg[...], a[...])
        landing.wait()
        e_in = (dot_nt(g_ref[...], w[...]) + thin) * gain_ref[...].astype(F32)
        mean = jnp.mean(e_in * n, axis=-1, keepdims=True)
        result = mg[...] + scale * (e_in - n * mean)
        kept[...] = result[:block]
        back[...] = result[block:].astype(BF16)

    return kernel_call(
        body, place, bundle, landing,
        [(v, VM) for v in (g, hgrad, x, mid_grad, gain, inner)],
        [(like((2, block, width), F32), one_of_pair(block, width)), (like((block, width), BF16), VM)],
        [], "qkv_backward", time=0.2, ties=ties,
    )


def complete(place, partial, back, ties, name):
    _, block, width = partial.shape

    def kernel(place_ref, partial_ref, back_ref, *rest):
        rest[-1][...] = back_ref[...].astype(partial.dtype)

    return pl.pallas_call(
        kernel,
        out_shape=jax.ShapeDtypeStruct(partial.shape, partial.dtype),
        grid_spec=pltpu.PrefetchScalarGridSpec(
            num_scalar_prefetch=1,
            grid=(1,),
            in_specs=[pl.BlockSpec(memory_space=pltpu.HBM), pl.BlockSpec(memory_space=pltpu.VMEM)]
            + [pl.BlockSpec(memory_space=pltpu.HBM)] * len(ties),
            out_specs=pl.BlockSpec((None, block, width), lambda i, p: (1 - p[0] // 2, 0, 0)),
        ),
        input_output_aliases={1: 0},
        compiler_params=pltpu.CompilerParams(vmem_limit_bytes=64 * 2**20),
        cost_estimate=work(0.5),
        name=name,
    )(place, partial, back, *ties)


def pack_factors(place, inners, outers):
    widths = [a.shape[0] for a in inners] + [b.shape[1] for b in outers]
    n = len(inners)
    mix = outers[0].shape[0]
    narrow = (n + 1, n + 2)

    def body(pr, land_refs, ins, outs, weights, sems, scratch):
        for which, out in enumerate(outs):
            row = lax.broadcasted_iota(jnp.int32, (RANK, mix), 0) + pr[3 + which] * RANK
            choose = (row == lax.broadcasted_iota(jnp.int32, (RANK, mix), 1)).astype(F32).astype(BF16)
            at = 0
            for i, ref in enumerate(ins):
                part = dot_nt(choose, ref[...]) if i < n or i in narrow else dot(choose, ref[...])
                out[:, at : at + widths[i]] = part.astype(BF16)
                at += widths[i]

    shape = (like((RANK, sum(widths)), BF16), VM)
    return kernel_call(
        body, place, NO_BUNDLE, [], [(v.T if i in narrow else v, VM) for i, v in enumerate((*inners, *outers))],
        [shape, shape], [], "pack_factors",
    )


def unpack_factors(place, slots, widths, chunks):
    inner_w, outer_w = widths[:7], widths[7:]
    width, kv = 4 * outer_w[0], 4 * outer_w[1]
    part = outer_w[4] // chunks
    starts = [sum(widths[:i]) for i in range(len(widths))]

    def body(pr, land_refs, ins, outs, weights, sems, scratch):
        iq, oq, io, oo, igl, ogl, da, db = outs
        (nat,) = scratch
        mine, two, got = ins
        nat[pr[0]] = mine[...]
        nat[pr[0] ^ 2] = two[...]
        nat[pr[0] ^ 1] = got[:RANK]
        nat[pr[0] ^ 3] = got[RANK:]
        oq[...] = jnp.zeros(oq.shape, BF16)
        for t in range(4):
            get = lambda i, a=0, n=None: nat[t, :, starts[i] + a : starts[i] + a + (n or widths[i])]
            w = inner_w[0]
            here = slice(t * w, (t + 1) * w)
            for i in range(3):
                iq[i * RANK : (i + 1) * RANK, here] = get(i)
            io[:, here] = get(3)
            igl[:RANK, here] = get(4)
            igl[RANK:, here] = get(5)
            base = 0
            for i in range(3):
                n = outer_w[i]
                oq[i * RANK : (i + 1) * RANK, base + t * n : base + (t + 1) * n] = get(7 + i)
                base += 4 * n
            oo[:, here] = get(10)
            db[:, here] = get(13)
            for u in range(chunks):
                there = slice(t * part, (t + 1) * part)
                ogl[u, :RANK, there] = get(11, u * part, part)
                ogl[u, RANK:, there] = get(12, u * part, part)
                da[u, :, there] = get(6, u * part, part)

    shapes = [
        (3 * RANK, width), (3 * RANK, width + 2 * kv), (RANK, width), (RANK, width), (2 * RANK, width),
        (chunks, 2 * RANK, 4 * part), (chunks, RANK, 4 * part), (RANK, width),
    ]
    return kernel_call(
        body, place, NO_BUNDLE, [], [(v, VM) for v in slots], [(like(sh, BF16), VM) for sh in shapes],
        [pltpu.VMEM((4, *slots[0].shape), BF16)], "unpack_factors",
    )


def fold_cores(place, sums, name, ties=()):
    n = len(sums)
    cols = sum(k.shape[2] for k, _ in sums)

    def body(pr, land_refs, ins, outs, weights, sems, scratch):
        chip = pr[0] // 2
        for out, which in zip(outs, (chip, 1 - chip)):
            at = 0
            for keep_ref, got_ref in zip(ins[:n], ins[n:]):
                w = keep_ref.shape[2]
                out[:, at : at + w] = (keep_ref[which] + got_ref[which].astype(F32)).astype(BF16)
                at += w
            out[:, cols:] = jnp.full((RANK, LANES), pr[3], jnp.int32).astype(F32).astype(BF16)

    shape = (like((RANK, cols + LANES), BF16), VM)
    return kernel_call(
        body, place, NO_BUNDLE, [], [(k, VM) for k, _ in sums] + [(g, VM) for _, g in sums],
        [shape, shape], [], name, ties=ties,
    )


def spread_sums(place, groups, pieces, mix, name, ties=()):
    count = sum(v.shape[0] for v in groups[0])
    tall = [len(g) > 1 for g in groups]

    def body(pr, land_refs, ins, outs, weights, sems, scratch):
        gots, at, held = [], 0, list(scratch)
        for g in groups:
            refs = ins[at : at + len(g)]
            at += len(g)
            if len(g) == 1:
                gots.append(refs[0])
                continue
            got, row = held.pop(0), 0
            for ref in refs:
                got[row : row + ref.shape[0]] = ref[...]
                row += ref.shape[0]
            gots.append(got)
        tag = gots[0][:, -LANES:].astype(F32).astype(jnp.int32) * RANK
        spot = tag + lax.broadcasted_iota(jnp.int32, (count, LANES), 0) % RANK
        choose = (spot == lax.broadcasted_iota(jnp.int32, (count, LANES), 1)).astype(F32).astype(BF16)
        choose_t = choose.T
        for out, (is_inner, runs) in zip(outs, pieces):
            at = 0
            for g, start, n in runs:
                if is_inner:
                    out[at : at + n] = dot_tn(gots[g][:, start : start + n], choose)
                else:
                    out[:, at : at + n] = dot(choose_t, gots[g][:, start : start + n])
                at += n

    outs = []
    for is_inner, runs in pieces:
        n = sum(c for _, _, c in runs)
        outs.append((like((n, mix) if is_inner else (mix, n), F32), VM))
    scratch = [pltpu.VMEM((count, g[0].shape[1]), BF16) for g, t in zip(groups, tall) if t]
    return kernel_call(
        body, place, NO_BUNDLE, [], [(v, VM) for g in groups for v in g], outs, scratch, name, ties=ties
    )


def local(
    tokens,
    cotangent,
    prefix_len,
    adapter_index,
    gain_attn,
    gain_mlp,
    query_weight,
    key_weight,
    value_weight,
    output_weight,
    gate_weight,
    lift_weight,
    drop_weight,
    *factors,
):
    _, block, width = tokens.shape
    rep, shard = lax.axis_index("rep"), lax.axis_index("shard")
    chip = shard // 2
    rows = 2 * block
    kv_width = KV_HEADS * HEAD_DIM
    where = jnp.stack([shard, rep % 4]).astype(jnp.int32)
    place = jnp.concatenate(
        [where, jnp.stack([prefix_len[chip], adapter_index[chip], adapter_index[1 - chip]])]
    )

    weights = (query_weight, key_weight, value_weight, output_weight, gate_weight, lift_weight, drop_weight)
    inners, outers = factors[0::2], factors[1::2]
    widths = [a.shape[0] for a in inners] + [b.shape[1] for b in outers]
    chunks = 4
    ff = gate_weight.shape[1]
    bundles = make_bundles(width, kv_width, ff, chunks, 4)
    positions = jnp.concatenate(
        [shard * block + jnp.arange(block), (shard ^ 2) * block + jnp.arange(block)]
    )
    cos_table, sine_table = rotary_tables(positions.astype(F32), HEAD_DIM)
    cos_full = jnp.concatenate([cos_table, cos_table], axis=1)
    sin_full = jnp.concatenate([-sine_table, sine_table], axis=1)
    gain_one, gain_two = gain_attn[None], gain_mlp[None]
    cos_t, sin_t = cos_table.T, sine_table.T

    relay = Relay(where, weights, bundles)
    half = block // 2
    near = {i: to_core(weights[i]) for i in (4, 5, 6)}
    relay.step()
    mine, others = pack_factors(place, inners, outers)
    slot_two = to_chip(others)
    (tokens_a,), _ = relay.step([(tokens, 0, half)], ties=(near[4], near[5], sin_full, cos_full, cos_t, sin_t, gain_one, gain_two, place))
    (tokens_b,), _ = relay.step([(tokens, half, half)], ties=(slot_two,))
    joined = join(mine, slot_two)
    got = to_core(joined)
    relay.step(ties=(near[6], got))
    inner_qkv, outer_qkv, inner_o, outer_o, inner_gl, outer_gl, drop_a, drop_b = unpack_factors(
        place, (mine, slot_two, got), widths, chunks
    )

    def landing(i):
        return landing_operands(bundles[i], weights, near, relay.here[i], relay.there[i])

    (cot_a,), begun = relay.step([(cotangent, 0, half)], ties=(inner_qkv,), across=False)
    queries, kv_own, hidden_qkv, normed_attn, x = qkv_forward(
        place, bundles[0], landing(0), tokens, (tokens_a, tokens_b), gain_one,
        inner_qkv, outer_qkv, cos_full, sin_full, begun[:1],
    )
    (cot_b,), begun = relay.step([(cotangent, half, half)], ties=(x,))
    kv_own = gate(kv_own, begun[:1])
    relay.across(1, begun[:1])
    kv_near = to_core(kv_own)
    heads_out, lse = attend(place, queries, kv_own, kv_near)
    middle, normed_mlp, attended, output_hidden, cot, hidden_gl, hidden_d = out_forward(
        place, bundles[1], landing(1), heads_out, x, gain_two, inner_o, outer_o,
        cotangent, (cot_a, cot_b), inner_gl, drop_b,
    )
    relay.step(ties=(normed_mlp,))
    sums, kept_sums = None, []
    for u in range(chunks):
        *sums, keep, send = mlp_chunk(
            place, bundles[2 + u], landing(2 + u), normed_mlp, cot, hidden_gl, hidden_d,
            outer_gl, drop_a, u, sums, f"mlp_{u}",
        )
        kept_sums.append((keep, to_core(send)))
        if u < 2:
            relay.step(ties=(keep,))
    early = fold_cores(place, kept_sums[:-1], "fold_early", (keep,))
    mixed_kept, mixed_back, middle_grad, grad_heads, keep, send = out_backward(
        place, bundles[1], landing(1), sums, middle, cot, gain_two, normed_mlp, attended,
        output_hidden, (drop_b, inner_gl, inner_o, outer_o), early[:1],
    )

    mixed_back = to_chip(mixed_back)
    early = join(early[0], to_chip(early[1]))
    folded = fold_cores(place, [kept_sums[-1], (keep, to_core(send))], "fold_late")
    parts, halves = [], 2
    for i in range(halves):
        dq, dkv, dkv_send = attend_back(
            place, queries, kv_own, kv_near, grad_heads, lse, cos_t, sin_t, i, halves,
            folded if i else (early,),
        )
        if i:
            late = to_chip(folded[1])
            dkv_send = gate(dkv_send, (late, mixed_back))
        parts.append((dq, dkv, to_core(dkv_send)))
    early = lax.all_gather(early, "rep", axis=0, tiled=True)
    late_both = join(folded[0], late, ties=parts[0][:1])
    late = lax.all_gather(late_both, "rep", axis=0, tiled=True)
    g, hgrad, keep, send = qkv_gradients(
        place, parts, cos_full, sin_full, normed_attn, hidden_qkv, outer_qkv, (late_both,)
    )
    folded = fold_cores(place, [(keep, to_core(send))], "fold_first")
    other = to_chip(folded[1])
    both = join(folded[0], other)
    input_kept, input_back = qkv_backward(
        place, bundles[0], landing(0), g, hgrad, x, middle_grad, gain_one, inner_qkv, (both, early)
    )
    line = [both]
    for k in range(2, lax.axis_size("rep"), 2):
        line.append(move(both, lambda r, s, k=k: (r ^ k, s)))
    line = join(*line, ties=(input_back,))
    input_back = to_chip(gate(input_back, (line,)))
    first = [line, to_y(line)]
    mixed = complete(place, mixed_kept, mixed_back, (), "complete_mixed")

    mix = ADAPTERS * RANK
    w, kw = width // 4, kv_width // 4
    part = ff // 4 // chunks
    wide = 3 * part
    runs = lambda j: [
        (0, u * wide + j * part, part) if u < chunks - 1 else (1, j * part, part) for u in range(chunks)
    ]
    rest = lambda j: [(1, wide + j * w, w)]
    g_out, l_out, d_in, d_out, g_in, l_in, o_in, o_out = spread_sums(
        place, [[early], [late]],
        [(False, runs(0)), (False, runs(1)), (True, runs(2)), (False, rest(0)), (True, rest(1)),
         (True, rest(2)), (True, rest(3)), (False, rest(4))],
        mix, "spread_late",
    )
    q_in, k_in, v_in, q_out, k_out, v_out = spread_sums(
        place, [first],
        [(True, [(0, 0, w)]), (True, [(0, w, w)]), (True, [(0, 2 * w, w)]), (False, [(0, 3 * w, w)]),
         (True, [(0, 4 * w, kw)]), (True, [(0, 4 * w + kw, kw)])],
        mix, "spread_first", (o_out,),
    )
    k_out, v_out = k_out.T, v_out.T
    input_grad = complete(place, input_kept, input_back, (q_in,), "complete_input_grad")
    return (mixed, input_grad, q_in, q_out, k_in, k_out, v_in, v_out, o_in, o_out,
            g_in, g_out, l_in, l_out, d_in, d_out)


def solution(mesh):
    token_place = P("rep", "shard", None)
    row, col = P("shard", None), P(None, "shard")
    return jax.shard_map(
        local,
        mesh=mesh,
        in_specs=(token_place, token_place, P("rep"), P("rep"), P(), P()) + (row,) * 7 + (row, col) * 7,
        out_specs=(token_place, token_place) + (row, col) * 7,
        check_vma=False,
    )
```

profile of v0, /device:TPU:0, one launch (start us, length us, event | category | flops | bytes accessed | tf_op | source)
XLA Modules:
  0.0 441.6 jit_solution(1596679888755065513)
XLA Ops:
  8.9 2.6 pack_0.1
  11.5 2.6 collective-permute-start
  19.2 2.5 concatenate.17.refs_11_.place_ref.place
  24.9 3.5 collective-permute-done.refs_2_.refs_5_.refs_3_
  28.4 3.0 pack_1.1
  36.2 3.8 pack_factors.1
  40.7 13.0 %collective-permute-done.6.refs_8_.refs_1_ = bf16[16,6912]{1,0:T(8,128)(2,1)} collective-permute-done((bf16[16,6912]{1,0:T(8,128)(2,1)}, bf16[16,6912]{1,0:T(8,128)(2,1)}, u32[]{:S(2)}, u32[]{:S(2)}) %collective-permute-start.6) | collective-permute-done | bytes 221216 | tf_op jit(solution)/shard_map/ppermute | solution.py:32
  53.7 3.6 pack_2.1
  63.8 2.1 collective-permute-done.11.refs_8_.refs_2_
  65.9 10.1 %collective-permute-done.7.refs_6_.refs_7_.refs_2_ = bf16[720,512]{1,0:T(8,128)(2,1)} collective-permute-done((bf16[720,512]{1,0:T(8,128)(2,1)}, bf16[720,512]{1,0:T(8,128)(2,1)}, u32[]{:S(2)}, u32[]{:S(2)}) %collective-permute-start.7) | collective-permute-done | bytes 737312 | tf_op jit(solution)/shard_map/ppermute | solution.py:32
  77.3 3.0 collective-permute-done.8.refs_3_.refs_5_.refs_7_.refs_0_
  80.2 3.3 pack_3.1
  83.5 5.2 %across_0.1.refs_3_ = bf16[4608,512]{1,0:T(8,128)(2,1)} custom-call(s32[2]{0:T(128)} %pad_add_fusion.place_ref, bf16[384,1536]{1,0:T(8,128)(2,1)} %refs_0_.33, bf16[384,768]{1,0:T(8,128)(2,1)} %refs_1_.27, bf16[384,768]{1,0:T(8,128)(2,1)} %refs_2_.25, bf16[576,512]{1,0:T(8,128)(2,1)} %collective-permute-done.refs_2_.refs_5_.refs_3_, ...), custom_call_target="tpu_custom_call" | custom-call | flops 110000000 | bytes 1048576 | tf_op jit(solution)/shard_map/across_0/pallas_call | solution.py:159
  93.3 3.0 unpack_factors.1
  96.3 8.6 %collective-permute-done.12.refs_6_.refs_3_ = bf16[576,512]{1,0:T(8,128)(2,1)} collective-permute-done((bf16[576,512]{1,0:T(8,128)(2,1)}, bf16[576,512]{1,0:T(8,128)(2,1)}, u32[]{:S(2)}, u32[]{:S(2)}) %collective-permute-start.12) | collective-permute-done | bytes 589856 | tf_op jit(solution)/shard_map/ppermute | solution.py:32
  107.3 3.7 pack_4.1
  113.5 31.1 %qkv_forward.1 = (bf16[16,512,128]{2,1,0:T(8,128)(2,1)}, bf16[16,512,128]{2,1,0:T(8,128)(2,1)}, bf16[512,48]{1,0:T(8,128)(2,1)}, bf16[512,1536]{1,0:T(8,128)(2,1)}, bf16[512,1536]{1,0:T(8,128)(2,1)}) custom-call(s32[5]{0:T(128)} %concatenate.17.refs_11_.place_ref.place, bf16[384,1536]{1,0:T(8,128)(2,1)} %refs_0_.33, bf16[384,768]{1,0:T(8,128)(2,1)} %refs_1_.27, ...), custom_call_target="tpu_custom_call" | custom-call | flops 5500000256 | bytes 1048576 | tf_op jit(solution)/shard_map/qkv_forward/pallas_call | solution.py:671
  144.6 3.7 pack_5.1
  148.4 3.6 across_1.1.refs_1_
  156.2 3.8 across_2.1.refs_6_
  160.1 14.8 %attend.1 = (bf16[16,512,128]{2,1,0:T(8,128)(2,1)}, f32[8,2,512]{2,1,0:T(2,128)}) custom-call(s32[5]{0:T(128)} %concatenate.17.refs_11_.place_ref.place, bf16[16,512,128]{2,1,0:T(8,128)(2,1)} %get-tuple-element.137.q, bf16[16,512,128]{2,1,0:T(8,128)(2,1)} %gate.3.k_own.v_own, bf16[16,512,128]{2,1,0:T(8,128)(2,1)} %collective-permute-done.23.k_near.v_near, ...), custom_call_target="tpu_custom_call" | custom-call | flops 5500000256 | bytes 1048576 | tf_op jit(solution)/shard_map/attend/pallas_call | solution.py:503
  176.6 14.6 %out_forward.1 = (f32[512,1536]{1,0:T(8,128)}, bf16[512,1536]{1,0:T(8,128)(2,1)}, bf16[512,1536]{1,0:T(8,128)(2,1)}, bf16[512,16]{1,0:T(8,128)(2,1)}, bf16[512,1...) custom-call(s32[5]{0:T(128)} %concatenate.17.refs_11_.place_ref.place, ...), custom_call_target="tpu_custom_call" | custom-call | flops 5500000256 | bytes 1048576 | tf_op jit(solution)/shard_map/out_forward/pallas_call | solution.py:671
  191.2 2.9 pack_6.1
  194.2 3.8 across_3.1.refs_6_
  201.2 21.2 %mlp_0.1 = (f32[512,1536]{1,0:T(8,128)}, f32[512,1536]{1,0:T(8,128)}, f32[3,512,16]{2,1,0:T(8,128)}, f32[2,16,768]{2,1,0:T(8,128)}, bf16[2,16,768]{2,1,0:T(8,128)(2,1)}) custom-call(s32[5]{0:T(128)} %concatenate.17.refs_11_.place_ref.place, bf16[384,4096]{1,0:T(8,128)(2,1)} %refs_0_.31, bf16[384,4096]{1,0:T(8,128)(2,1)} %refs_1_.26, ...), custom_call_target="tpu_custom_call" | custom-call | flops 5500000256 | bytes 1048576 | tf_op jit(solution)/shard_map/mlp_0/pallas_call | solution.py:671
  222.5 2.7 pack_7.1
  226.5 3.8 across_4.1.refs_6_
  230.4 23.0 %mlp_1.1 = (f32[512,1536]{1,0:T(8,128)}, f32[512,1536]{1,0:T(8,128)}, f32[3,512,16]{2,1,0:T(8,128)}, f32[2,16,768]{2,1,0:T(8,128)}, bf16[2,16,768]{2,1,0:T(8,128)(2,1)}) custom-call(s32[5]{0:T(128)} %concatenate.17.refs_11_.place_ref.place, bf16[384,4096]{1,0:T(8,128)(2,1)} %refs_0_.31, bf16[384,4096]{1,0:T(8,128)(2,1)} %refs_1_.26, ...), custom_call_target="tpu_custom_call" | custom-call | flops 5500000256 | bytes 1048576 | tf_op jit(solution)/shard_map/mlp_1/pallas_call | solution.py:671
  253.4 3.8 across_5.1.refs_6_
  258.3 23.1 %mlp_2.1 = (f32[512,1536]{1,0:T(8,128)}, f32[512,1536]{1,0:T(8,128)}, f32[3,512,16]{2,1,0:T(8,128)}, f32[2,16,768]{2,1,0:T(8,128)}, bf16[2,16,768]{2,1,0:T(8,128)(2,1)}) custom-call(s32[5]{0:T(128)} %concatenate.17.refs_11_.place_ref.place, bf16[384,4096]{1,0:T(8,128)(2,1)} %refs_0_.31, bf16[384,4096]{1,0:T(8,128)(2,1)} %refs_1_.26, ...), custom_call_target="tpu_custom_call" | custom-call | flops 5500000256 | bytes 1048576 | tf_op jit(solution)/shard_map/mlp_2/pallas_call | solution.py:671
  281.6 23.3 %mlp_3.1 = (f32[512,1536]{1,0:T(8,128)}, f32[512,1536]{1,0:T(8,128)}, f32[3,512,16]{2,1,0:T(8,128)}, f32[2,16,768]{2,1,0:T(8,128)}, bf16[2,16,768]{2,1,0:T(8,128)(2,1)}) custom-call(s32[5]{0:T(128)} %concatenate.17.refs_11_.place_ref.place, bf16[384,4096]{1,0:T(8,128)(2,1)} %refs_0_.31, bf16[384,4096]{1,0:T(8,128)(2,1)} %refs_1_.26, ...), custom_call_target="tpu_custom_call" | custom-call | flops 5500000256 | bytes 1048576 | tf_op jit(solution)/shard_map/mlp_3/pallas_call | solution.py:671
  304.9 2.4 fold_early.1
  307.9 4.5 %collective-permute-done.36.refs_1_ = bf16[16,2432]{1,0:T(8,128)(2,1)} collective-permute-done((bf16[16,2432]{1,0:T(8,128)(2,1)}, bf16[16,2432]{1,0:T(8,128)(2,1)}, u32[]{:S(2)}, u32[]{:S(2)}) %collective-permute-start.36) | collective-permute-done | bytes 77856 | tf_op jit(solution)/shard_map/ppermute | solution.py:32
  314.0 15.0 %out_backward.1 = (bf16[2,256,1536]{2,1,0:T(8,128)(2,1)}, bf16[256,1536]{1,0:T(8,128)(2,1)}, f32[512,1536]{1,0:T(8,128)}, bf16[16,512,128]{2,1,0:T(8,128)(2,1)},...) custom-call(s32[5]{0:T(128)} %concatenate.17.refs_11_.place_ref.place, bf16[384,1536]{1,0:T(8,128)(2,1)} %refs_0_.32, ...), custom_call_target="tpu_custom_call" | custom-call | flops 16499999744 | bytes 1048576 | tf_op jit(solution)/shard_map/out_backward/pallas_call | solution.py:671
  331.3 2.5 fold_late.1
  335.4 14.1 %attend_back_0.1 = (bf16[8,512,128]{2,1,0:T(8,128)(2,1)}, f32[2,4,512,128]{3,2,1,0:T(8,128)}, bf16[2,4,512,128]{3,2,1,0:T(8,128)(2,1)}) custom-call(s32[5]{0:T(128)} %concatenate.17.refs_11_.place_ref.place, bf16[16,512,128]{2,1,0:T(8,128)(2,1)} %get-tuple-element.137.q, bf16[16,512,128]{2,1,0:T(8,128)(2,1)} %gate.3.k_own.v_own, ...), custom_call_target="tpu_custom_call" | custom-call | flops 1100000000 | bytes 1048576 | tf_op jit(solution)/shard_map/attend_back_0/pallas_call | solution.py:584
  352.1 13.8 %attend_back_1.1 = (bf16[8,512,128]{2,1,0:T(8,128)(2,1)}, f32[2,4,512,128]{3,2,1,0:T(8,128)}, bf16[2,4,512,128]{3,2,1,0:T(8,128)(2,1)}) custom-call(s32[5]{0:T(128)} %concatenate.17.refs_11_.place_ref.place, bf16[16,512,128]{2,1,0:T(8,128)(2,1)} %get-tuple-element.137.q, bf16[16,512,128]{2,1,0:T(8,128)(2,1)} %gate.3.k_own.v_own, ...), custom_call_target="tpu_custom_call" | custom-call | flops 1100000000 | bytes 1048576 | tf_op jit(solution)/shard_map/attend_back_1/pallas_call | solution.py:584
  366.5 2.6 collective-permute-done.41.refs_5_
  369.2 10.5 %qkv_gradients.1 = (bf16[512,3072]{1,0:T(8,128)(2,1)}, bf16[512,48]{1,0:T(8,128)(2,1)}, f32[2,16,1920]{2,1,0:T(8,128)}, bf16[2,16,1920]{2,1,0:T(8,128)(2,1)}) custom-call(s32[5]{0:T(128)} %concatenate.17.refs_11_.place_ref.place, bf16[8,512,128]{2,1,0:T(8,128)(2,1)} %get-tuple-element.182.refs_2_.refs_0_, f32[2,4,512,128]{3,2,1,0:T(8,128)} %get-tuple-element.183.refs_1_, ...), custom_call_target="tpu_custom_call" | custom-call | flops 1100000000 | bytes 1048576 | tf_op jit(solution)/shard_map/qkv_gradients/pallas_call | solution.py:671
  381.4 2.4 fold_first.1
  384.4 4.2 collective-permute-done.43.refs_1_
  390.2 3.6 collective-permute-start.46
  394.5 14.9 %qkv_backward.1 = (f32[2,256,1536]{2,1,0:T(8,128)}, bf16[256,1536]{1,0:T(8,128)(2,1)}) custom-call(s32[5]{0:T(128)} %concatenate.17.refs_11_.place_ref.place, bf16[384,1536]{1,0:T(8,128)(2,1)} %refs_0_.33, bf16[384,768]{1,0:T(8,128)(2,1)} %refs_1_.27, bf16[384,768]{1,0:T(8,128)(2,1)} %refs_2_.25, bf16[4608,512]{1,0:T(8,128)(2,1)} %across_0.1.refs_3_, ...), custom_call_target="tpu_custom_call" | custom-call | flops 220000000 | bytes 1048576 | tf_op jit(solution)/shard_map/qkv_backward/pallas_call | solution.py:671
  414.0 2.7 complete_mixed.1
  416.7 4.2 spread_late.1
  420.9 5.5 %collective-permute-done.48.refs_1_ = bf16[128,2048]{1,0:T(8,128)(2,1)} collective-permute-done((bf16[128,2048]{1,0:T(8,128)(2,1)}, bf16[128,2048]{1,0:T(8,128)(2,1)}, u32[]{:S(2)}, u32[]{:S(2)}) %collective-permute-start.48) | collective-permute-done | bytes 524320 | tf_op jit(solution)/shard_map/ppermute | solution.py:32
  426.4 3.2 spread_first.1
  431.5 3.0 complete_input_grad.1
  (112 shorter events, 65.0 us)
Async XLA Ops:
  7.2 387.4 %all-gather.3.cloned.1.call-start = ((), (), s32[]{:S(2)}) async-start(), calls=%async_computation | async-start | bytes 1400832 | tf_op jit(solution)/shard_map/all_gather | solution.py:1296
  7.2 21.1 %collective-permute-start.1 = (bf16[384,4096]{1,0:T(8,128)(2,1)}, bf16[384,4096]{1,0:T(8,128)(2,1)}, u32[]{:S(2)}, u32[]{:S(2)}) collective-permute-start(bf16[384,4096]{1,0:T(8,128)(2,1)} %refs_0_.31), channel_id=1, source_target_pairs={{0,1},{1,0},{2,3},{3,2},{4,5},{5,4},{6,7},{7,6},{8,9},{9,8},{10,11... | collective-permute-start | bytes 9437192 | tf_op jit(solution)/shard_map/ppermute | solution.py:32
  7.7 20.6 %collective-permute-start.2 = (bf16[384,4096]{1,0:T(8,128)(2,1)}, bf16[384,4096]{1,0:T(8,128)(2,1)}, u32[]{:S(2)}, u32[]{:S(2)}) collective-permute-start(bf16[384,4096]{1,0:T(8,128)(2,1)} %refs_1_.26), channel_id=1, source_target_pairs={{0,1},{1,0},{2,3},{3,2},{4,5},{5,4},{6,7},{7,6},{8,9},{9,8},{10,11... | collective-permute-start | bytes 9437192 | tf_op jit(solution)/shard_map/ppermute | solution.py:32
  7.8 58.1 %collective-permute-start.10 = (bf16[1024,1536]{1,0:T(8,128)(2,1)}, bf16[1024,1536]{1,0:T(8,128)(2,1)}, u32[]{:S(2)}, u32[]{:S(2)}) collective-permute-start(bf16[1024,1536]{1,0:T(8,128)(2,1)} %refs_2_.24), channel_id=1, source_target_pairs={{0,1},{1,0},{2,3},{3,2},{4,5},{5,4},{6,7},{7,6},{8,9},{9,8},{10,11... | collective-permute-start | bytes 9437192 | tf_op jit(solution)/shard_map/ppermute | solution.py:32
  11.5 16.9 %collective-permute-start = (bf16[576,512]{1,0:T(8,128)(2,1)}, bf16[576,512]{1,0:T(8,128)(2,1)}, u32[]{:S(2)}, u32[]{:S(2)}) collective-permute-start(bf16[576,512]{1,0:T(8,128)(2,1)} %pack_0.1), channel_id=1, source_target_pairs={{0,2},{1,3},{2,0},{3,1},{4,6},{5,7},{6,4},{7,5},{8,10},{9,11},{10,... | collective-permute-start | bytes 1769480 | tf_op jit(solution)/shard_map/ppermute | solution.py:32
  31.3 22.3 %collective-permute-start.3 = (bf16[672,512]{1,0:T(8,128)(2,1)}, bf16[672,512]{1,0:T(8,128)(2,1)}, u32[]{:S(2)}, u32[]{:S(2)}) collective-permute-start(bf16[672,512]{1,0:T(8,128)(2,1)} %get-tuple-element.117), channel_id=1, source_target_pairs={{0,2},{1,3},{2,0},{3,1},{4,6},{5,7},{6,4},{7,5},{8,10},{9,11},{10,... | collective-permute-start | bytes 2064392 | tf_op jit(solution)/shard_map/ppermute | solution.py:32
  33.2 20.5 %collective-permute-start.4 = (bf16[288,512]{1,0:T(8,128)(2,1)}, bf16[288,512]{1,0:T(8,128)(2,1)}, u32[]{:S(2)}, u32[]{:S(2)}) collective-permute-start(bf16[288,512]{1,0:T(8,128)(2,1)} %get-tuple-element.118), channel_id=1, source_target_pairs={{0,8},{1,9},{2,10},{3,11},{4,12},{5,13},{6,14},{7,15},{8,0},{9,1},... | collective-permute-start | bytes 884744 | tf_op jit(solution)/shard_map/ppermute | solution.py:32
  34.7 18.9 %collective-permute-start.5 = (bf16[288,512]{1,0:T(8,128)(2,1)}, bf16[288,512]{1,0:T(8,128)(2,1)}, u32[]{:S(2)}, u32[]{:S(2)}) collective-permute-start(bf16[288,512]{1,0:T(8,128)(2,1)} %get-tuple-element.119), channel_id=1, source_target_pairs={{0,4},{1,5},{2,6},{3,7},{4,0},{5,1},{6,2},{7,3},{8,12},{9,13},{10,... | collective-permute-start | bytes 884744 | tf_op jit(solution)/shard_map/ppermute | solution.py:32
  40.1 13.6 %collective-permute-start.6 = (bf16[16,6912]{1,0:T(8,128)(2,1)}, bf16[16,6912]{1,0:T(8,128)(2,1)}, u32[]{:S(2)}, u32[]{:S(2)}) collective-permute-start(bf16[16,6912]{1,0:T(8,128)(2,1)} %get-tuple-element.120), channel_id=1, source_target_pairs={{0,2},{1,3},{2,0},{3,1},{4,6},{5,7},{6,4},{7,5},{8,10},{9,11},{10,... | collective-permute-start | bytes 663560 | tf_op jit(solution)/shard_map/ppermute | solution.py:32
  57.2 23.0 %collective-permute-start.8 = (bf16[960,512]{1,0:T(8,128)(2,1)}, bf16[960,512]{1,0:T(8,128)(2,1)}, u32[]{:S(2)}, u32[]{:S(2)}) collective-permute-start(bf16[960,512]{1,0:T(8,128)(2,1)} %get-tuple-element.122), channel_id=1, source_target_pairs={{0,2},{1,3},{2,0},{3,1},{4,6},{5,7},{6,4},{7,5},{8,10},{9,11},{10,... | collective-permute-start | bytes 2949128 | tf_op jit(solution)/shard_map/ppermute | solution.py:32
  58.8 17.2 %collective-permute-start.7 = (bf16[720,512]{1,0:T(8,128)(2,1)}, bf16[720,512]{1,0:T(8,128)(2,1)}, u32[]{:S(2)}, u32[]{:S(2)}) collective-permute-start(bf16[720,512]{1,0:T(8,128)(2,1)} %get-tuple-element.121), channel_id=1, source_target_pairs={{0,4},{1,5},{2,6},{3,7},{4,0},{5,1},{6,2},{7,3},{8,12},{9,13},{10,... | collective-permute-start | bytes 2211848 | tf_op jit(solution)/shard_map/ppermute | solution.py:32
  60.4 16.9 %collective-permute-start.9 = (bf16[720,512]{1,0:T(8,128)(2,1)}, bf16[720,512]{1,0:T(8,128)(2,1)}, u32[]{:S(2)}, u32[]{:S(2)}) collective-permute-start(bf16[720,512]{1,0:T(8,128)(2,1)} %get-tuple-element.123), channel_id=1, source_target_pairs={{0,8},{1,9},{2,10},{3,11},{4,12},{5,13},{6,14},{7,15},{8,0},{9,1},... | collective-permute-start | bytes 2211848 | tf_op jit(solution)/shard_map/ppermute | solution.py:32
  63.8 2.1 collective-permute-start.11
  88.8 24.7 %collective-permute-start.18 = (bf16[4608,512]{1,0:T(8,128)(2,1)}, bf16[4608,512]{1,0:T(8,128)(2,1)}, u32[]{:S(2)}, u32[]{:S(2)}) collective-permute-start(bf16[4608,512]{1,0:T(8,128)(2,1)} %across_0.1.refs_3_), channel_id=1, source_target_pairs={{0,1},{1,0},{2,3},{3,2},{4,5},{5,4},{6,7},{7,6},{8,9},{9,8},{10,11... | collective-permute-start | bytes 14155784 | tf_op jit(solution)/shard_map/ppermute | solution.py:32
  88.8 16.1 %collective-permute-start.12 = (bf16[576,512]{1,0:T(8,128)(2,1)}, bf16[576,512]{1,0:T(8,128)(2,1)}, u32[]{:S(2)}, u32[]{:S(2)}) collective-permute-start(bf16[576,512]{1,0:T(8,128)(2,1)} %get-tuple-element.125), channel_id=1, source_target_pairs={{0,8},{1,9},{2,10},{3,11},{4,12},{5,13},{6,14},{7,15},{8,0},{9,1},... | collective-permute-start | bytes 1769480 | tf_op jit(solution)/shard_map/ppermute | solution.py:32
  90.3 15.7 %collective-permute-start.13 = (bf16[576,512]{1,0:T(8,128)(2,1)}, bf16[576,512]{1,0:T(8,128)(2,1)}, u32[]{:S(2)}, u32[]{:S(2)}) collective-permute-start(bf16[576,512]{1,0:T(8,128)(2,1)} %get-tuple-element.126), channel_id=1, source_target_pairs={{0,4},{1,5},{2,6},{3,7},{4,0},{5,1},{6,2},{7,3},{8,12},{9,13},{10,... | collective-permute-start | bytes 1769480 | tf_op jit(solution)/shard_map/ppermute | solution.py:32
  91.8 15.4 %collective-permute-start.14 = (bf16[576,512]{1,0:T(8,128)(2,1)}, bf16[576,512]{1,0:T(8,128)(2,1)}, u32[]{:S(2)}, u32[]{:S(2)}) collective-permute-start(bf16[576,512]{1,0:T(8,128)(2,1)} %get-tuple-element.127.refs_8_), channel_id=1, source_target_pairs={{0,2},{1,3},{2,0},{3,1},{4,6},{5,7},{6,4},{7,5},{8,10},{9,11},{10,... | collective-permute-start | bytes 1769480 | tf_op jit(solution)/shard_map/ppermute | solution.py:32
  111.0 33.6 %collective-permute-start.15 = (bf16[960,512]{1,0:T(8,128)(2,1)}, bf16[960,512]{1,0:T(8,128)(2,1)}, u32[]{:S(2)}, u32[]{:S(2)}) collective-permute-start(bf16[960,512]{1,0:T(8,128)(2,1)} %get-tuple-element.129.refs_13_), channel_id=1, source_target_pairs={{0,2},{1,3},{2,0},{3,1},{4,6},{5,7},{6,4},{7,5},{8,10},{9,11},{10,... | collective-permute-start | bytes 2949128 | tf_op jit(solution)/shard_map/ppermute | solution.py:32
  112.5 32.1 %collective-permute-start.16 = (bf16[864,512]{1,0:T(8,128)(2,1)}, bf16[864,512]{1,0:T(8,128)(2,1)}, u32[]{:S(2)}, u32[]{:S(2)}) collective-permute-start(bf16[864,512]{1,0:T(8,128)(2,1)} %get-tuple-element.130), channel_id=1, source_target_pairs={{0,8},{1,9},{2,10},{3,11},{4,12},{5,13},{6,14},{7,15},{8,0},{9,1},... | collective-permute-start | bytes 2654216 | tf_op jit(solution)/shard_map/ppermute | solution.py:32
  113.0 31.6 %collective-permute-start.17 = (bf16[864,512]{1,0:T(8,128)(2,1)}, bf16[864,512]{1,0:T(8,128)(2,1)}, u32[]{:S(2)}, u32[]{:S(2)}) collective-permute-start(bf16[864,512]{1,0:T(8,128)(2,1)} %get-tuple-element.131), channel_id=1, source_target_pairs={{0,4},{1,5},{2,6},{3,7},{4,0},{5,1},{6,2},{7,3},{8,12},{9,13},{10,... | collective-permute-start | bytes 2654216 | tf_op jit(solution)/shard_map/ppermute | solution.py:32
  148.3 11.7 %collective-permute-start.23 = (bf16[16,512,128]{2,1,0:T(8,128)(2,1)}, bf16[16,512,128]{2,1,0:T(8,128)(2,1)}, u32[]{:S(2)}, u32[]{:S(2)}) collective-permute-start(bf16[16,512,128]{2,1,0:T(8,128)(2,1)} %gate.3.k_own.v_own), channel_id=1, source_target_pairs={{0,1},{1,0},{2,3},{3,2},{4,5},{5,4},{6,7},{7,6},{8,9},{9,8},{10,11... | collective-permute-start | bytes 6291464 | tf_op jit(solution)/shard_map/ppermute | solution.py:32
  152.0 24.6 %collective-permute-start.19 = (bf16[2304,512]{1,0:T(8,128)(2,1)}, bf16[2304,512]{1,0:T(8,128)(2,1)}, u32[]{:S(2)}, u32[]{:S(2)}) collective-permute-start(bf16[2304,512]{1,0:T(8,128)(2,1)} %across_1.1.refs_1_), channel_id=1, source_target_pairs={{0,1},{1,0},{2,3},{3,2},{4,5},{5,4},{6,7},{7,6},{8,9},{9,8},{10,11... | collective-permute-start | bytes 7077896 | tf_op jit(solution)/shard_map/ppermute | solution.py:32
  152.6 24.1 %collective-permute-start.20 = (bf16[960,512]{1,0:T(8,128)(2,1)}, bf16[960,512]{1,0:T(8,128)(2,1)}, u32[]{:S(2)}, u32[]{:S(2)}) collective-permute-start(bf16[960,512]{1,0:T(8,128)(2,1)} %get-tuple-element.134.refs_6_.refs_1_.refs_5_), channel_id=1, source_target_pairs={{0,2},{1,3},{2,0},{3,1},{4,6},{5,7},{6,4},{7,5},{8,10},{9,11},{10,... | collective-permute-start | bytes 2949128 | tf_op jit(solution)/shard_map/ppermute | solution.py:32
  153.3 37.9 %collective-permute-start.21 = (bf16[864,512]{1,0:T(8,128)(2,1)}, bf16[864,512]{1,0:T(8,128)(2,1)}, u32[]{:S(2)}, u32[]{:S(2)}) collective-permute-start(bf16[864,512]{1,0:T(8,128)(2,1)} %get-tuple-element.135), channel_id=1, source_target_pairs={{0,8},{1,9},{2,10},{3,11},{4,12},{5,13},{6,14},{7,15},{8,0},{9,1},... | collective-permute-start | bytes 2654216 | tf_op jit(solution)/shard_map/ppermute | solution.py:32
  154.7 36.5 %collective-permute-start.22 = (bf16[864,512]{1,0:T(8,128)(2,1)}, bf16[864,512]{1,0:T(8,128)(2,1)}, u32[]{:S(2)}, u32[]{:S(2)}) collective-permute-start(bf16[864,512]{1,0:T(8,128)(2,1)} %get-tuple-element.136), channel_id=1, source_target_pairs={{0,4},{1,5},{2,6},{3,7},{4,0},{5,1},{6,2},{7,3},{8,12},{9,13},{10,... | collective-permute-start | bytes 2654216 | tf_op jit(solution)/shard_map/ppermute | solution.py:32
  160.0 41.2 %collective-permute-start.26 = (bf16[2304,512]{1,0:T(8,128)(2,1)}, bf16[2304,512]{1,0:T(8,128)(2,1)}, u32[]{:S(2)}, u32[]{:S(2)}) collective-permute-start(bf16[2304,512]{1,0:T(8,128)(2,1)} %across_2.1.refs_6_), channel_id=1, source_target_pairs={{0,1},{1,0},{2,3},{3,2},{4,5},{5,4},{6,7},{7,6},{8,9},{9,8},{10,11... | collective-permute-start | bytes 7077896 | tf_op jit(solution)/shard_map/ppermute | solution.py:32
  198.0 32.4 %collective-permute-start.29 = (bf16[2304,512]{1,0:T(8,128)(2,1)}, bf16[2304,512]{1,0:T(8,128)(2,1)}, u32[]{:S(2)}, u32[]{:S(2)}) collective-permute-start(bf16[2304,512]{1,0:T(8,128)(2,1)} %across_3.1.refs_6_), channel_id=1, source_target_pairs={{0,1},{1,0},{2,3},{3,2},{4,5},{5,4},{6,7},{7,6},{8,9},{9,8},{10,11... | collective-permute-start | bytes 7077896 | tf_op jit(solution)/shard_map/ppermute | solution.py:32
  198.1 24.4 %collective-permute-start.25 = (bf16[864,512]{1,0:T(8,128)(2,1)}, bf16[864,512]{1,0:T(8,128)(2,1)}, u32[]{:S(2)}, u32[]{:S(2)}) collective-permute-start(bf16[864,512]{1,0:T(8,128)(2,1)} %get-tuple-element.146), channel_id=1, source_target_pairs={{0,8},{1,9},{2,10},{3,11},{4,12},{5,13},{6,14},{7,15},{8,0},{9,1},... | collective-permute-start | bytes 2654216 | tf_op jit(solution)/shard_map/ppermute | solution.py:32
  199.8 22.7 %collective-permute-start.24 = (bf16[864,512]{1,0:T(8,128)(2,1)}, bf16[864,512]{1,0:T(8,128)(2,1)}, u32[]{:S(2)}, u32[]{:S(2)}) collective-permute-start(bf16[864,512]{1,0:T(8,128)(2,1)} %get-tuple-element.145.refs_5_), channel_id=1, source_target_pairs={{0,4},{1,5},{2,6},{3,7},{4,0},{5,1},{6,2},{7,3},{8,12},{9,13},{10,... | collective-permute-start | bytes 2654216 | tf_op jit(solution)/shard_map/ppermute | solution.py:32
  225.2 28.2 %collective-permute-start.27 = (bf16[576,512]{1,0:T(8,128)(2,1)}, bf16[576,512]{1,0:T(8,128)(2,1)}, u32[]{:S(2)}, u32[]{:S(2)}) collective-permute-start(bf16[576,512]{1,0:T(8,128)(2,1)} %get-tuple-element.153), channel_id=1, source_target_pairs={{0,8},{1,9},{2,10},{3,11},{4,12},{5,13},{6,14},{7,15},{8,0},{9,1},... | collective-permute-start | bytes 1769480 | tf_op jit(solution)/shard_map/ppermute | solution.py:32
  225.8 27.6 %collective-permute-start.28 = (bf16[576,512]{1,0:T(8,128)(2,1)}, bf16[576,512]{1,0:T(8,128)(2,1)}, u32[]{:S(2)}, u32[]{:S(2)}) collective-permute-start(bf16[576,512]{1,0:T(8,128)(2,1)} %get-tuple-element.154.refs_5_), channel_id=1, source_target_pairs={{0,4},{1,5},{2,6},{3,7},{4,0},{5,1},{6,2},{7,3},{8,12},{9,13},{10,... | collective-permute-start | bytes 1769480 | tf_op jit(solution)/shard_map/ppermute | solution.py:32
  230.3 27.9 %collective-permute-start.31 = (bf16[2304,512]{1,0:T(8,128)(2,1)}, bf16[2304,512]{1,0:T(8,128)(2,1)}, u32[]{:S(2)}, u32[]{:S(2)}) collective-permute-start(bf16[2304,512]{1,0:T(8,128)(2,1)} %across_4.1.refs_6_), channel_id=1, source_target_pairs={{0,1},{1,0},{2,3},{3,2},{4,5},{5,4},{6,7},{7,6},{8,9},{9,8},{10,11... | collective-permute-start | bytes 7077896 | tf_op jit(solution)/shard_map/ppermute | solution.py:32
  257.2 24.4 %collective-permute-start.30 = (bf16[2304,512]{1,0:T(8,128)(2,1)}, bf16[2304,512]{1,0:T(8,128)(2,1)}, u32[]{:S(2)}, u32[]{:S(2)}) collective-permute-start(bf16[2304,512]{1,0:T(8,128)(2,1)} %across_5.1.refs_6_), channel_id=1, source_target_pairs={{0,1},{1,0},{2,3},{3,2},{4,5},{5,4},{6,7},{7,6},{8,9},{9,8},{10,11... | collective-permute-start | bytes 7077896 | tf_op jit(solution)/shard_map/ppermute | solution.py:32
  257.8 47.1 %collective-permute-start.32 = (bf16[2,16,768]{2,1,0:T(8,128)(2,1)}, bf16[2,16,768]{2,1,0:T(8,128)(2,1)}, u32[]{:S(2)}, u32[]{:S(2)}) collective-permute-start(bf16[2,16,768]{2,1,0:T(8,128)(2,1)} %get-tuple-element.172), channel_id=1, source_target_pairs={{0,1},{1,0},{2,3},{3,2},{4,5},{5,4},{6,7},{7,6},{8,9},{9,8},{10,11... | collective-permute-start | bytes 147464 | tf_op jit(solution)/shard_map/ppermute | solution.py:32
  257.8 47.0 %collective-permute-start.33 = (bf16[2,16,768]{2,1,0:T(8,128)(2,1)}, bf16[2,16,768]{2,1,0:T(8,128)(2,1)}, u32[]{:S(2)}, u32[]{:S(2)}) collective-permute-start(bf16[2,16,768]{2,1,0:T(8,128)(2,1)} %get-tuple-element.173), channel_id=1, source_target_pairs={{0,1},{1,0},{2,3},{3,2},{4,5},{5,4},{6,7},{7,6},{8,9},{9,8},{10,11... | collective-permute-start | bytes 147464 | tf_op jit(solution)/shard_map/ppermute | solution.py:32
  281.4 23.5 %collective-permute-start.34 = (bf16[2,16,768]{2,1,0:T(8,128)(2,1)}, bf16[2,16,768]{2,1,0:T(8,128)(2,1)}, u32[]{:S(2)}, u32[]{:S(2)}) collective-permute-start(bf16[2,16,768]{2,1,0:T(8,128)(2,1)} %get-tuple-element.174), channel_id=1, source_target_pairs={{0,1},{1,0},{2,3},{3,2},{4,5},{5,4},{6,7},{7,6},{8,9},{9,8},{10,11... | collective-permute-start | bytes 147464 | tf_op jit(solution)/shard_map/ppermute | solution.py:32
  307.3 5.1 %collective-permute-start.36 = (bf16[16,2432]{1,0:T(8,128)(2,1)}, bf16[16,2432]{1,0:T(8,128)(2,1)}, u32[]{:S(2)}, u32[]{:S(2)}) collective-permute-start(bf16[16,2432]{1,0:T(8,128)(2,1)} %get-tuple-element.181), channel_id=1, source_target_pairs={{0,2},{1,3},{2,0},{3,1},{4,6},{5,7},{6,4},{7,5},{8,10},{9,11},{10,... | collective-permute-start | bytes 233480 | tf_op jit(solution)/shard_map/ppermute | solution.py:32
  314.0 102.7 %all-gather.5.cloned.1.call-start = ((), (), s32[]{:S(2)}) async-start(), calls=%async_computation.1 | async-start | bytes 1622016 | tf_op jit(solution)/shard_map/all_gather | solution.py:1298
  329.0 36.9 %collective-permute-start.35 = (bf16[256,1536]{1,0:T(8,128)(2,1)}, bf16[256,1536]{1,0:T(8,128)(2,1)}, u32[]{:S(2)}, u32[]{:S(2)}) collective-permute-start(bf16[256,1536]{1,0:T(8,128)(2,1)} %get-tuple-element.178), channel_id=1, source_target_pairs={{0,2},{1,3},{2,0},{3,1},{4,6},{5,7},{6,4},{7,5},{8,10},{9,11},{10,... | collective-permute-start | bytes 2359304 | tf_op jit(solution)/shard_map/ppermute | solution.py:32
  333.8 16.6 %collective-permute-start.40 = (bf16[16,2816]{1,0:T(8,128)(2,1)}, bf16[16,2816]{1,0:T(8,128)(2,1)}, u32[]{:S(2)}, u32[]{:S(2)}) collective-permute-start(bf16[16,2816]{1,0:T(8,128)(2,1)} %get-tuple-element.189.rest_1_), channel_id=1, source_target_pairs={{0,2},{1,3},{2,0},{3,1},{4,6},{5,7},{6,4},{7,5},{8,10},{9,11},{10,... | collective-permute-start | bytes 270344 | tf_op jit(solution)/shard_map/ppermute | solution.py:32
  352.0 14.5 %collective-permute-start.37 = (bf16[2,4,512,128]{3,2,1,0:T(8,128)(2,1)}, bf16[2,4,512,128]{3,2,1,0:T(8,128)(2,1)}, u32[]{:S(2)}, u32[]{:S(2)}) collective-permute-start(bf16[2,4,512,128]{3,2,1,0:T(8,128)(2,1)} %get-tuple-element.184), channel_id=1, source_target_pairs={{0,1},{1,0},{2,3},{3,2},{4,5},{5,4},{6,7},{7,6},{8,9},{9,8},{10,11... | collective-permute-start | bytes 3145736 | tf_op jit(solution)/shard_map/ppermute | solution.py:32
  366.0 3.2 collective-permute-start.41
  383.9 4.7 %collective-permute-start.43 = (bf16[16,2048]{1,0:T(8,128)(2,1)}, bf16[16,2048]{1,0:T(8,128)(2,1)}, u32[]{:S(2)}, u32[]{:S(2)}) collective-permute-start(bf16[16,2048]{1,0:T(8,128)(2,1)} %get-tuple-element.201), channel_id=1, source_target_pairs={{0,2},{1,3},{2,0},{3,1},{4,6},{5,7},{6,4},{7,5},{8,10},{9,11},{10,... | collective-permute-start | bytes 196616 | tf_op jit(solution)/shard_map/ppermute | solution.py:32
  390.2 19.4 %collective-permute-start.46 = (bf16[32,2048]{1,0:T(8,128)(2,1)}, bf16[32,2048]{1,0:T(8,128)(2,1)}, u32[]{:S(2)}, u32[]{:S(2)}) collective-permute-start(bf16[32,2048]{1,0:T(8,128)(2,1)} %join.8.refs_11_.refs_0_), channel_id=1, source_target_pairs={{0,24},{1,25},{2,26},{3,27},{4,28},{5,29},{6,30},{7,31},{8,16},{9,... | collective-permute-start | bytes 393224 | tf_op jit(solution)/shard_map/ppermute | solution.py:32
  393.7 16.3 %collective-permute-start.45 = (bf16[32,2048]{1,0:T(8,128)(2,1)}, bf16[32,2048]{1,0:T(8,128)(2,1)}, u32[]{:S(2)}, u32[]{:S(2)}) collective-permute-start(bf16[32,2048]{1,0:T(8,128)(2,1)} %join.8.refs_11_.refs_0_), channel_id=1, source_target_pairs={{0,16},{1,17},{2,18},{3,19},{4,20},{5,21},{6,22},{7,23},{8,24},{9,... | collective-permute-start | bytes 393224 | tf_op jit(solution)/shard_map/ppermute | solution.py:32
  393.8 16.3 %collective-permute-start.44 = (bf16[32,2048]{1,0:T(8,128)(2,1)}, bf16[32,2048]{1,0:T(8,128)(2,1)}, u32[]{:S(2)}, u32[]{:S(2)}) collective-permute-start(bf16[32,2048]{1,0:T(8,128)(2,1)} %join.8.refs_11_.refs_0_), channel_id=1, source_target_pairs={{0,8},{1,9},{2,10},{3,11},{4,12},{5,13},{6,14},{7,15},{8,0},{9,1},... | collective-permute-start | bytes 393224 | tf_op jit(solution)/shard_map/ppermute | solution.py:32
  412.0 19.5 %collective-permute-start.47 = (bf16[256,1536]{1,0:T(8,128)(2,1)}, bf16[256,1536]{1,0:T(8,128)(2,1)}, u32[]{:S(2)}, u32[]{:S(2)}) collective-permute-start(bf16[256,1536]{1,0:T(8,128)(2,1)} %gate.5), channel_id=1, source_target_pairs={{0,2},{1,3},{2,0},{3,1},{4,6},{5,7},{6,4},{7,5},{8,10},{9,11},{10,... | collective-permute-start | bytes 2359304 | tf_op jit(solution)/shard_map/ppermute | solution.py:32
  412.9 13.5 %collective-permute-start.48 = (bf16[128,2048]{1,0:T(8,128)(2,1)}, bf16[128,2048]{1,0:T(8,128)(2,1)}, u32[]{:S(2)}, u32[]{:S(2)}) collective-permute-start(bf16[128,2048]{1,0:T(8,128)(2,1)} %join.9.refs_1_.refs_0_), channel_id=1, source_target_pairs={{0,4},{1,5},{2,6},{3,7},{4,0},{5,1},{6,2},{7,3},{8,12},{9,13},{10,... | collective-permute-start | bytes 1572872 | tf_op jit(solution)/shard_map/ppermute | solution.py:32
  (3 other events, 5.3 us)
Sparse Core Ops, SparseCore 0:
  314.1 41.4 all-gather.2
  358.4 49.2 all-gather.4
where the time goes:
time: 446 us; the launch traced here: 442 us
  Pallas kernels  305 us (68%)
  waiting for transfers between devices  68.5 us (15%)
  starting transfers between devices  42.4 us (10%)
  between operations  14.7 us (3%)
  local copies, waits for them, and re-layouts  7.66 us (2%)
    pallas_call x16, Pallas kernels, kernel_call(): pl.pallas_call(kernel, out_shape=[o for o, _ in outs], grid_spec=pltpu.Pr...  198 us
    ppermute x49, waiting for transfers between devices, move(): return lax.ppermute(value, AXES, pairs)  68.4 us
    pallas_call x14, Pallas kernels, pack(): pl.pallas_call(kernel, out_shape=[jax.ShapeDtypeStruct(sh, BF16) for sh i...  49.4 us
    ppermute x49, starting transfers between devices, move(): return lax.ppermute(value, AXES, pairs)  42.3 us
    pallas_call x2, Pallas kernels, attend_back(): pl.pallas_call(functools.partial(attend_back_kernel, scale=HEAD_DIM ** (-...  27.9 us
    pallas_call x1, Pallas kernels, attend(): pl.pallas_call(functools.partial(attend_kernel, scale=HEAD_DIM ** (-0.5))...  14.8 us
  transfers between devices with their start and end apart: 51, of which 19 were waited for; matrix products, arithmetic and copies ran while one was open for 3% of the time, Pallas kernels for 65%

commit v1 on v0

--- a/solution.py
+++ b/solution.py
@@ -1281,7 +1281,7 @@
     )
 
     mixed_back = to_chip(mixed_back)
-    early = join(early[0], to_chip(early[1]))
+    early = join(early[0], to_chip(early[1]), ties=(grad_heads,))
     folded = fold_cores(place, [kept_sums[-1], (keep, to_core(send))], "fold_late")
     parts, halves = [], 2
     for i in range(halves):

time: 446 us -> 443 us (level)
  waiting for transfers between devices: 68.5 us -> 62.9 us
    ppermute x49, waiting for transfers between devices: 68.4 us -> 62.9 us  [move(): return lax.ppermute(value, AXES, pairs)]
  transfers between devices with their start and end apart: 51 -> 51, of which waited for: 19 -> 18; matrix products, arithmetic and copies ran while one was open for 3% -> 3% of each run, Pallas kernels for 65% -> 65%
where the time goes in v1:
time: 443 us; the launch traced here: 438 us
  Pallas kernels  305 us (69%)
  waiting for transfers between devices  62.9 us (14%)
  starting transfers between devices  44.3 us (10%)
  between operations  14.7 us (3%)
  local copies, waits for them, and re-layouts  7.66 us (2%)
    pallas_call x16, Pallas kernels, kernel_call(): pl.pallas_call(kernel, out_shape=[o for o, _ in outs], grid_spec=pltpu.Pr...  198 us
    ppermute x49, waiting for transfers between devices, move(): return lax.ppermute(value, AXES, pairs)  62.9 us
    pallas_call x14, Pallas kernels, pack(): pl.pallas_call(kernel, out_shape=[jax.ShapeDtypeStruct(sh, BF16) for sh i...  49.4 us
    ppermute x49, starting transfers between devices, move(): return lax.ppermute(value, AXES, pairs)  44.2 us
    pallas_call x2, Pallas kernels, attend_back(): pl.pallas_call(functools.partial(attend_back_kernel, scale=HEAD_DIM ** (-...  28 us
    pallas_call x1, Pallas kernels, attend(): pl.pallas_call(functools.partial(attend_kernel, scale=HEAD_DIM ** (-0.5))...  14.8 us
  transfers between devices with their start and end apart: 51, of which 18 were waited for; matrix products, arithmetic and copies ran while one was open for 3% of the time, Pallas kernels for 65%

profile of v1, /device:TPU:0, one launch (start us, length us, event | category | flops | bytes accessed | tf_op | source)
XLA Modules:
  0.0 438.0 jit_solution(8355616371833791898)
XLA Ops:
  8.9 2.6 pack_0.1
  11.5 2.6 collective-permute-start
  19.2 2.5 concatenate.17.refs_11_.place_ref.place
  24.9 3.5 collective-permute-done.refs_2_.refs_5_.refs_3_
  28.4 3.0 pack_1.1
  36.2 3.8 pack_factors.1
  40.7 13.0 %collective-permute-done.6.refs_8_.refs_1_ = bf16[16,6912]{1,0:T(8,128)(2,1)} collective-permute-done((bf16[16,6912]{1,0:T(8,128)(2,1)}, bf16[16,6912]{1,0:T(8,128)(2,1)}, u32[]{:S(2)}, u32[]{:S(2)}) %collective-permute-start.6) | collective-permute-done | bytes 221216 | tf_op jit(solution)/shard_map/ppermute | solution.py:32
  53.7 3.6 pack_2.1
  63.8 2.1 collective-permute-done.11.refs_8_.refs_2_
  65.9 10.1 %collective-permute-done.7.refs_6_.refs_7_.refs_2_ = bf16[720,512]{1,0:T(8,128)(2,1)} collective-permute-done((bf16[720,512]{1,0:T(8,128)(2,1)}, bf16[720,512]{1,0:T(8,128)(2,1)}, u32[]{:S(2)}, u32[]{:S(2)}) %collective-permute-start.7) | collective-permute-done | bytes 737312 | tf_op jit(solution)/shard_map/ppermute | solution.py:32
  77.3 3.0 collective-permute-done.8.refs_3_.refs_5_.refs_7_.refs_0_
  80.3 3.3 pack_3.1
  83.5 5.2 %across_0.1.refs_3_ = bf16[4608,512]{1,0:T(8,128)(2,1)} custom-call(s32[2]{0:T(128)} %pad_add_fusion.place_ref, bf16[384,1536]{1,0:T(8,128)(2,1)} %refs_0_.33, bf16[384,768]{1,0:T(8,128)(2,1)} %refs_1_.27, bf16[384,768]{1,0:T(8,128)(2,1)} %refs_2_.25, bf16[576,512]{1,0:T(8,128)(2,1)} %collective-permute-done.refs_2_.refs_5_.refs_3_, ...), custom_call_target="tpu_custom_call" | custom-call | flops 110000000 | bytes 1048576 | tf_op jit(solution)/shard_map/across_0/pallas_call | solution.py:159
  93.3 3.0 unpack_factors.1
  96.3 8.6 %collective-permute-done.12.refs_6_.refs_3_ = bf16[576,512]{1,0:T(8,128)(2,1)} collective-permute-done((bf16[576,512]{1,0:T(8,128)(2,1)}, bf16[576,512]{1,0:T(8,128)(2,1)}, u32[]{:S(2)}, u32[]{:S(2)}) %collective-permute-start.12) | collective-permute-done | bytes 589856 | tf_op jit(solution)/shard_map/ppermute | solution.py:32
  107.3 3.7 pack_4.1
  113.5 31.1 %qkv_forward.1 = (bf16[16,512,128]{2,1,0:T(8,128)(2,1)}, bf16[16,512,128]{2,1,0:T(8,128)(2,1)}, bf16[512,48]{1,0:T(8,128)(2,1)}, bf16[512,1536]{1,0:T(8,128)(2,1)}, bf16[512,1536]{1,0:T(8,128)(2,1)}) custom-call(s32[5]{0:T(128)} %concatenate.17.refs_11_.place_ref.place, bf16[384,1536]{1,0:T(8,128)(2,1)} %refs_0_.33, bf16[384,768]{1,0:T(8,128)(2,1)} %refs_1_.27, ...), custom_call_target="tpu_custom_call" | custom-call | flops 5500000256 | bytes 1048576 | tf_op jit(solution)/shard_map/qkv_forward/pallas_call | solution.py:671
  144.6 3.7 pack_5.1
  148.4 3.6 across_1.1.refs_1_
  156.2 3.8 across_2.1.refs_6_
  160.1 14.8 %attend.1 = (bf16[16,512,128]{2,1,0:T(8,128)(2,1)}, f32[8,2,512]{2,1,0:T(2,128)}) custom-call(s32[5]{0:T(128)} %concatenate.17.refs_11_.place_ref.place, bf16[16,512,128]{2,1,0:T(8,128)(2,1)} %get-tuple-element.137.q, bf16[16,512,128]{2,1,0:T(8,128)(2,1)} %gate.3.k_own.v_own, bf16[16,512,128]{2,1,0:T(8,128)(2,1)} %collective-permute-done.23.k_near.v_near, ...), custom_call_target="tpu_custom_call" | custom-call | flops 5500000256 | bytes 1048576 | tf_op jit(solution)/shard_map/attend/pallas_call | solution.py:503
  176.6 14.6 %out_forward.1 = (f32[512,1536]{1,0:T(8,128)}, bf16[512,1536]{1,0:T(8,128)(2,1)}, bf16[512,1536]{1,0:T(8,128)(2,1)}, bf16[512,16]{1,0:T(8,128)(2,1)}, bf16[512,1...) custom-call(s32[5]{0:T(128)} %concatenate.17.refs_11_.place_ref.place, ...), custom_call_target="tpu_custom_call" | custom-call | flops 5500000256 | bytes 1048576 | tf_op jit(solution)/shard_map/out_forward/pallas_call | solution.py:671
  191.2 2.9 pack_6.1
  194.2 3.8 across_3.1.refs_6_
  201.2 21.2 %mlp_0.1 = (f32[512,1536]{1,0:T(8,128)}, f32[512,1536]{1,0:T(8,128)}, f32[3,512,16]{2,1,0:T(8,128)}, f32[2,16,768]{2,1,0:T(8,128)}, bf16[2,16,768]{2,1,0:T(8,128)(2,1)}) custom-call(s32[5]{0:T(128)} %concatenate.17.refs_11_.place_ref.place, bf16[384,4096]{1,0:T(8,128)(2,1)} %refs_0_.31, bf16[384,4096]{1,0:T(8,128)(2,1)} %refs_1_.26, ...), custom_call_target="tpu_custom_call" | custom-call | flops 5500000256 | bytes 1048576 | tf_op jit(solution)/shard_map/mlp_0/pallas_call | solution.py:671
  222.5 2.7 pack_7.1
  226.5 3.8 across_4.1.refs_6_
  230.4 23.0 %mlp_1.1 = (f32[512,1536]{1,0:T(8,128)}, f32[512,1536]{1,0:T(8,128)}, f32[3,512,16]{2,1,0:T(8,128)}, f32[2,16,768]{2,1,0:T(8,128)}, bf16[2,16,768]{2,1,0:T(8,128)(2,1)}) custom-call(s32[5]{0:T(128)} %concatenate.17.refs_11_.place_ref.place, bf16[384,4096]{1,0:T(8,128)(2,1)} %refs_0_.31, bf16[384,4096]{1,0:T(8,128)(2,1)} %refs_1_.26, ...), custom_call_target="tpu_custom_call" | custom-call | flops 5500000256 | bytes 1048576 | tf_op jit(solution)/shard_map/mlp_1/pallas_call | solution.py:671
  253.4 3.8 across_5.1.refs_6_
  258.3 23.1 %mlp_2.1 = (f32[512,1536]{1,0:T(8,128)}, f32[512,1536]{1,0:T(8,128)}, f32[3,512,16]{2,1,0:T(8,128)}, f32[2,16,768]{2,1,0:T(8,128)}, bf16[2,16,768]{2,1,0:T(8,128)(2,1)}) custom-call(s32[5]{0:T(128)} %concatenate.17.refs_11_.place_ref.place, bf16[384,4096]{1,0:T(8,128)(2,1)} %refs_0_.31, bf16[384,4096]{1,0:T(8,128)(2,1)} %refs_1_.26, ...), custom_call_target="tpu_custom_call" | custom-call | flops 5500000256 | bytes 1048576 | tf_op jit(solution)/shard_map/mlp_2/pallas_call | solution.py:671
  281.6 23.3 %mlp_3.1 = (f32[512,1536]{1,0:T(8,128)}, f32[512,1536]{1,0:T(8,128)}, f32[3,512,16]{2,1,0:T(8,128)}, f32[2,16,768]{2,1,0:T(8,128)}, bf16[2,16,768]{2,1,0:T(8,128)(2,1)}) custom-call(s32[5]{0:T(128)} %concatenate.17.refs_11_.place_ref.place, bf16[384,4096]{1,0:T(8,128)(2,1)} %refs_0_.31, bf16[384,4096]{1,0:T(8,128)(2,1)} %refs_1_.26, ...), custom_call_target="tpu_custom_call" | custom-call | flops 5500000256 | bytes 1048576 | tf_op jit(solution)/shard_map/mlp_3/pallas_call | solution.py:671
  304.9 2.4 fold_early.1
  307.9 14.8 %out_backward.1 = (bf16[2,256,1536]{2,1,0:T(8,128)(2,1)}, bf16[256,1536]{1,0:T(8,128)(2,1)}, f32[512,1536]{1,0:T(8,128)}, bf16[16,512,128]{2,1,0:T(8,128)(2,1)},...) custom-call(s32[5]{0:T(128)} %concatenate.17.refs_11_.place_ref.place, bf16[384,1536]{1,0:T(8,128)(2,1)} %refs_0_.32, ...), custom_call_target="tpu_custom_call" | custom-call | flops 16499999744 | bytes 1048576 | tf_op jit(solution)/shard_map/out_backward/pallas_call | solution.py:671
  327.7 2.5 fold_late.1
  330.8 14.1 %attend_back_0.1 = (bf16[8,512,128]{2,1,0:T(8,128)(2,1)}, f32[2,4,512,128]{3,2,1,0:T(8,128)}, bf16[2,4,512,128]{3,2,1,0:T(8,128)(2,1)}) custom-call(s32[5]{0:T(128)} %concatenate.17.refs_11_.place_ref.place, bf16[16,512,128]{2,1,0:T(8,128)(2,1)} %get-tuple-element.137.q, bf16[16,512,128]{2,1,0:T(8,128)(2,1)} %gate.3.k_own.v_own, ...), custom_call_target="tpu_custom_call" | custom-call | flops 1100000000 | bytes 1048576 | tf_op jit(solution)/shard_map/attend_back_0/pallas_call | solution.py:584
  348.1 13.9 %attend_back_1.1 = (bf16[8,512,128]{2,1,0:T(8,128)(2,1)}, f32[2,4,512,128]{3,2,1,0:T(8,128)}, bf16[2,4,512,128]{3,2,1,0:T(8,128)(2,1)}) custom-call(s32[5]{0:T(128)} %concatenate.17.refs_11_.place_ref.place, bf16[16,512,128]{2,1,0:T(8,128)(2,1)} %get-tuple-element.137.q, bf16[16,512,128]{2,1,0:T(8,128)(2,1)} %gate.3.k_own.v_own, ...), custom_call_target="tpu_custom_call" | custom-call | flops 1100000000 | bytes 1048576 | tf_op jit(solution)/shard_map/attend_back_1/pallas_call | solution.py:584
  362.6 2.6 collective-permute-done.41.refs_5_
  365.3 10.5 %qkv_gradients.1 = (bf16[512,3072]{1,0:T(8,128)(2,1)}, bf16[512,48]{1,0:T(8,128)(2,1)}, f32[2,16,1920]{2,1,0:T(8,128)}, bf16[2,16,1920]{2,1,0:T(8,128)(2,1)}) custom-call(s32[5]{0:T(128)} %concatenate.17.refs_11_.place_ref.place, bf16[8,512,128]{2,1,0:T(8,128)(2,1)} %get-tuple-element.182.refs_2_.refs_0_, f32[2,4,512,128]{3,2,1,0:T(8,128)} %get-tuple-element.183.refs_1_, ...), custom_call_target="tpu_custom_call" | custom-call | flops 1100000000 | bytes 1048576 | tf_op jit(solution)/shard_map/qkv_gradients/pallas_call | solution.py:671
  377.5 2.4 fold_first.1
  381.3 3.3 collective-permute-done.43.refs_1_
  386.2 3.6 collective-permute-start.46
  390.6 15.1 %qkv_backward.1 = (f32[2,256,1536]{2,1,0:T(8,128)}, bf16[256,1536]{1,0:T(8,128)(2,1)}) custom-call(s32[5]{0:T(128)} %concatenate.17.refs_11_.place_ref.place, bf16[384,1536]{1,0:T(8,128)(2,1)} %refs_0_.33, bf16[384,768]{1,0:T(8,128)(2,1)} %refs_1_.27, bf16[384,768]{1,0:T(8,128)(2,1)} %refs_2_.25, bf16[4608,512]{1,0:T(8,128)(2,1)} %across_0.1.refs_3_, ...), custom_call_target="tpu_custom_call" | custom-call | flops 220000000 | bytes 1048576 | tf_op jit(solution)/shard_map/qkv_backward/pallas_call | solution.py:671
  405.7 4.4 %collective-permute-done.45.refs_2_ = bf16[32,2048]{1,0:T(8,128)(2,1)} collective-permute-done((bf16[32,2048]{1,0:T(8,128)(2,1)}, bf16[32,2048]{1,0:T(8,128)(2,1)}, u32[]{:S(2)}, u32[]{:S(2)}) %collective-permute-start.45) | collective-permute-done | bytes 131104 | tf_op jit(solution)/shard_map/ppermute | solution.py:32
  410.1 1.9 join.9.refs_1_.refs_0_
  414.9 2.7 complete_mixed.1
  417.6 4.2 spread_late.1
  423.5 3.2 spread_first.1
  427.9 3.0 complete_input_grad.1
  (112 shorter events, 65.9 us)
Async XLA Ops:
  7.2 383.4 %all-gather.3.cloned.1.call-start = ((), (), s32[]{:S(2)}) async-start(), calls=%async_computation | async-start | bytes 1400832 | tf_op jit(solution)/shard_map/all_gather | solution.py:1296
  7.2 21.1 %collective-permute-start.1 = (bf16[384,4096]{1,0:T(8,128)(2,1)}, bf16[384,4096]{1,0:T(8,128)(2,1)}, u32[]{:S(2)}, u32[]{:S(2)}) collective-permute-start(bf16[384,4096]{1,0:T(8,128)(2,1)} %refs_0_.31), channel_id=1, source_target_pairs={{0,1},{1,0},{2,3},{3,2},{4,5},{5,4},{6,7},{7,6},{8,9},{9,8},{10,11... | collective-permute-start | bytes 9437192 | tf_op jit(solution)/shard_map/ppermute | solution.py:32
  7.7 20.6 %collective-permute-start.2 = (bf16[384,4096]{1,0:T(8,128)(2,1)}, bf16[384,4096]{1,0:T(8,128)(2,1)}, u32[]{:S(2)}, u32[]{:S(2)}) collective-permute-start(bf16[384,4096]{1,0:T(8,128)(2,1)} %refs_1_.26), channel_id=1, source_target_pairs={{0,1},{1,0},{2,3},{3,2},{4,5},{5,4},{6,7},{7,6},{8,9},{9,8},{10,11... | collective-permute-start | bytes 9437192 | tf_op jit(solution)/shard_map/ppermute | solution.py:32
  7.8 58.1 %collective-permute-start.10 = (bf16[1024,1536]{1,0:T(8,128)(2,1)}, bf16[1024,1536]{1,0:T(8,128)(2,1)}, u32[]{:S(2)}, u32[]{:S(2)}) collective-permute-start(bf16[1024,1536]{1,0:T(8,128)(2,1)} %refs_2_.24), channel_id=1, source_target_pairs={{0,1},{1,0},{2,3},{3,2},{4,5},{5,4},{6,7},{7,6},{8,9},{9,8},{10,11... | collective-permute-start | bytes 9437192 | tf_op jit(solution)/shard_map/ppermute | solution.py:32
  11.5 16.9 %collective-permute-start = (bf16[576,512]{1,0:T(8,128)(2,1)}, bf16[576,512]{1,0:T(8,128)(2,1)}, u32[]{:S(2)}, u32[]{:S(2)}) collective-permute-start(bf16[576,512]{1,0:T(8,128)(2,1)} %pack_0.1), channel_id=1, source_target_pairs={{0,2},{1,3},{2,0},{3,1},{4,6},{5,7},{6,4},{7,5},{8,10},{9,11},{10,... | collective-permute-start | bytes 1769480 | tf_op jit(solution)/shard_map/ppermute | solution.py:32
  31.3 22.3 %collective-permute-start.3 = (bf16[672,512]{1,0:T(8,128)(2,1)}, bf16[672,512]{1,0:T(8,128)(2,1)}, u32[]{:S(2)}, u32[]{:S(2)}) collective-permute-start(bf16[672,512]{1,0:T(8,128)(2,1)} %get-tuple-element.117), channel_id=1, source_target_pairs={{0,2},{1,3},{2,0},{3,1},{4,6},{5,7},{6,4},{7,5},{8,10},{9,11},{10,... | collective-permute-start | bytes 2064392 | tf_op jit(solution)/shard_map/ppermute | solution.py:32
  33.2 20.5 %collective-permute-start.4 = (bf16[288,512]{1,0:T(8,128)(2,1)}, bf16[288,512]{1,0:T(8,128)(2,1)}, u32[]{:S(2)}, u32[]{:S(2)}) collective-permute-start(bf16[288,512]{1,0:T(8,128)(2,1)} %get-tuple-element.118), channel_id=1, source_target_pairs={{0,8},{1,9},{2,10},{3,11},{4,12},{5,13},{6,14},{7,15},{8,0},{9,1},... | collective-permute-start | bytes 884744 | tf_op jit(solution)/shard_map/ppermute | solution.py:32
  34.7 18.9 %collective-permute-start.5 = (bf16[288,512]{1,0:T(8,128)(2,1)}, bf16[288,512]{1,0:T(8,128)(2,1)}, u32[]{:S(2)}, u32[]{:S(2)}) collective-permute-start(bf16[288,512]{1,0:T(8,128)(2,1)} %get-tuple-element.119), channel_id=1, source_target_pairs={{0,4},{1,5},{2,6},{3,7},{4,0},{5,1},{6,2},{7,3},{8,12},{9,13},{10,... | collective-permute-start | bytes 884744 | tf_op jit(solution)/shard_map/ppermute | solution.py:32
  40.1 13.6 %collective-permute-start.6 = (bf16[16,6912]{1,0:T(8,128)(2,1)}, bf16[16,6912]{1,0:T(8,128)(2,1)}, u32[]{:S(2)}, u32[]{:S(2)}) collective-permute-start(bf16[16,6912]{1,0:T(8,128)(2,1)} %get-tuple-element.120), channel_id=1, source_target_pairs={{0,2},{1,3},{2,0},{3,1},{4,6},{5,7},{6,4},{7,5},{8,10},{9,11},{10,... | collective-permute-start | bytes 663560 | tf_op jit(solution)/shard_map/ppermute | solution.py:32
  57.2 23.0 %collective-permute-start.8 = (bf16[960,512]{1,0:T(8,128)(2,1)}, bf16[960,512]{1,0:T(8,128)(2,1)}, u32[]{:S(2)}, u32[]{:S(2)}) collective-permute-start(bf16[960,512]{1,0:T(8,128)(2,1)} %get-tuple-element.122), channel_id=1, source_target_pairs={{0,2},{1,3},{2,0},{3,1},{4,6},{5,7},{6,4},{7,5},{8,10},{9,11},{10,... | collective-permute-start | bytes 2949128 | tf_op jit(solution)/shard_map/ppermute | solution.py:32
  58.8 17.2 %collective-permute-start.7 = (bf16[720,512]{1,0:T(8,128)(2,1)}, bf16[720,512]{1,0:T(8,128)(2,1)}, u32[]{:S(2)}, u32[]{:S(2)}) collective-permute-start(bf16[720,512]{1,0:T(8,128)(2,1)} %get-tuple-element.121), channel_id=1, source_target_pairs={{0,4},{1,5},{2,6},{3,7},{4,0},{5,1},{6,2},{7,3},{8,12},{9,13},{10,... | collective-permute-start | bytes 2211848 | tf_op jit(solution)/shard_map/ppermute | solution.py:32
  60.4 16.9 %collective-permute-start.9 = (bf16[720,512]{1,0:T(8,128)(2,1)}, bf16[720,512]{1,0:T(8,128)(2,1)}, u32[]{:S(2)}, u32[]{:S(2)}) collective-permute-start(bf16[720,512]{1,0:T(8,128)(2,1)} %get-tuple-element.123), channel_id=1, source_target_pairs={{0,8},{1,9},{2,10},{3,11},{4,12},{5,13},{6,14},{7,15},{8,0},{9,1},... | collective-permute-start | bytes 2211848 | tf_op jit(solution)/shard_map/ppermute | solution.py:32
  63.8 2.1 collective-permute-start.11
  88.8 24.7 %collective-permute-start.18 = (bf16[4608,512]{1,0:T(8,128)(2,1)}, bf16[4608,512]{1,0:T(8,128)(2,1)}, u32[]{:S(2)}, u32[]{:S(2)}) collective-permute-start(bf16[4608,512]{1,0:T(8,128)(2,1)} %across_0.1.refs_3_), channel_id=1, source_target_pairs={{0,1},{1,0},{2,3},{3,2},{4,5},{5,4},{6,7},{7,6},{8,9},{9,8},{10,11... | collective-permute-start | bytes 14155784 | tf_op jit(solution)/shard_map/ppermute | solution.py:32
  88.8 16.1 %collective-permute-start.12 = (bf16[576,512]{1,0:T(8,128)(2,1)}, bf16[576,512]{1,0:T(8,128)(2,1)}, u32[]{:S(2)}, u32[]{:S(2)}) collective-permute-start(bf16[576,512]{1,0:T(8,128)(2,1)} %get-tuple-element.125), channel_id=1, source_target_pairs={{0,8},{1,9},{2,10},{3,11},{4,12},{5,13},{6,14},{7,15},{8,0},{9,1},... | collective-permute-start | bytes 1769480 | tf_op jit(solution)/shard_map/ppermute | solution.py:32
  90.3 15.7 %collective-permute-start.13 = (bf16[576,512]{1,0:T(8,128)(2,1)}, bf16[576,512]{1,0:T(8,128)(2,1)}, u32[]{:S(2)}, u32[]{:S(2)}) collective-permute-start(bf16[576,512]{1,0:T(8,128)(2,1)} %get-tuple-element.126), channel_id=1, source_target_pairs={{0,4},{1,5},{2,6},{3,7},{4,0},{5,1},{6,2},{7,3},{8,12},{9,13},{10,... | collective-permute-start | bytes 1769480 | tf_op jit(solution)/shard_map/ppermute | solution.py:32
  91.8 15.4 %collective-permute-start.14 = (bf16[576,512]{1,0:T(8,128)(2,1)}, bf16[576,512]{1,0:T(8,128)(2,1)}, u32[]{:S(2)}, u32[]{:S(2)}) collective-permute-start(bf16[576,512]{1,0:T(8,128)(2,1)} %get-tuple-element.127.refs_8_), channel_id=1, source_target_pairs={{0,2},{1,3},{2,0},{3,1},{4,6},{5,7},{6,4},{7,5},{8,10},{9,11},{10,... | collective-permute-start | bytes 1769480 | tf_op jit(solution)/shard_map/ppermute | solution.py:32
  111.0 33.6 %collective-permute-start.15 = (bf16[960,512]{1,0:T(8,128)(2,1)}, bf16[960,512]{1,0:T(8,128)(2,1)}, u32[]{:S(2)}, u32[]{:S(2)}) collective-permute-start(bf16[960,512]{1,0:T(8,128)(2,1)} %get-tuple-element.129.refs_13_), channel_id=1, source_target_pairs={{0,2},{1,3},{2,0},{3,1},{4,6},{5,7},{6,4},{7,5},{8,10},{9,11},{10,... | collective-permute-start | bytes 2949128 | tf_op jit(solution)/shard_map/ppermute | solution.py:32
  112.5 32.1 %collective-permute-start.16 = (bf16[864,512]{1,0:T(8,128)(2,1)}, bf16[864,512]{1,0:T(8,128)(2,1)}, u32[]{:S(2)}, u32[]{:S(2)}) collective-permute-start(bf16[864,512]{1,0:T(8,128)(2,1)} %get-tuple-element.130), channel_id=1, source_target_pairs={{0,8},{1,9},{2,10},{3,11},{4,12},{5,13},{6,14},{7,15},{8,0},{9,1},... | collective-permute-start | bytes 2654216 | tf_op jit(solution)/shard_map/ppermute | solution.py:32
  113.0 31.6 %collective-permute-start.17 = (bf16[864,512]{1,0:T(8,128)(2,1)}, bf16[864,512]{1,0:T(8,128)(2,1)}, u32[]{:S(2)}, u32[]{:S(2)}) collective-permute-start(bf16[864,512]{1,0:T(8,128)(2,1)} %get-tuple-element.131), channel_id=1, source_target_pairs={{0,4},{1,5},{2,6},{3,7},{4,0},{5,1},{6,2},{7,3},{8,12},{9,13},{10,... | collective-permute-start | bytes 2654216 | tf_op jit(solution)/shard_map/ppermute | solution.py:32
  148.3 11.7 %collective-permute-start.23 = (bf16[16,512,128]{2,1,0:T(8,128)(2,1)}, bf16[16,512,128]{2,1,0:T(8,128)(2,1)}, u32[]{:S(2)}, u32[]{:S(2)}) collective-permute-start(bf16[16,512,128]{2,1,0:T(8,128)(2,1)} %gate.3.k_own.v_own), channel_id=1, source_target_pairs={{0,1},{1,0},{2,3},{3,2},{4,5},{5,4},{6,7},{7,6},{8,9},{9,8},{10,11... | collective-permute-start | bytes 6291464 | tf_op jit(solution)/shard_map/ppermute | solution.py:32
  152.0 24.6 %collective-permute-start.19 = (bf16[2304,512]{1,0:T(8,128)(2,1)}, bf16[2304,512]{1,0:T(8,128)(2,1)}, u32[]{:S(2)}, u32[]{:S(2)}) collective-permute-start(bf16[2304,512]{1,0:T(8,128)(2,1)} %across_1.1.refs_1_), channel_id=1, source_target_pairs={{0,1},{1,0},{2,3},{3,2},{4,5},{5,4},{6,7},{7,6},{8,9},{9,8},{10,11... | collective-permute-start | bytes 7077896 | tf_op jit(solution)/shard_map/ppermute | solution.py:32
  152.6 24.1 %collective-permute-start.20 = (bf16[960,512]{1,0:T(8,128)(2,1)}, bf16[960,512]{1,0:T(8,128)(2,1)}, u32[]{:S(2)}, u32[]{:S(2)}) collective-permute-start(bf16[960,512]{1,0:T(8,128)(2,1)} %get-tuple-element.134.refs_6_.refs_1_.refs_5_), channel_id=1, source_target_pairs={{0,2},{1,3},{2,0},{3,1},{4,6},{5,7},{6,4},{7,5},{8,10},{9,11},{10,... | collective-permute-start | bytes 2949128 | tf_op jit(solution)/shard_map/ppermute | solution.py:32
  153.3 37.9 %collective-permute-start.21 = (bf16[864,512]{1,0:T(8,128)(2,1)}, bf16[864,512]{1,0:T(8,128)(2,1)}, u32[]{:S(2)}, u32[]{:S(2)}) collective-permute-start(bf16[864,512]{1,0:T(8,128)(2,1)} %get-tuple-element.135), channel_id=1, source_target_pairs={{0,8},{1,9},{2,10},{3,11},{4,12},{5,13},{6,14},{7,15},{8,0},{9,1},... | collective-permute-start | bytes 2654216 | tf_op jit(solution)/shard_map/ppermute | solution.py:32
  154.7 36.5 %collective-permute-start.22 = (bf16[864,512]{1,0:T(8,128)(2,1)}, bf16[864,512]{1,0:T(8,128)(2,1)}, u32[]{:S(2)}, u32[]{:S(2)}) collective-permute-start(bf16[864,512]{1,0:T(8,128)(2,1)} %get-tuple-element.136), channel_id=1, source_target_pairs={{0,4},{1,5},{2,6},{3,7},{4,0},{5,1},{6,2},{7,3},{8,12},{9,13},{10,... | collective-permute-start | bytes 2654216 | tf_op jit(solution)/shard_map/ppermute | solution.py:32
  160.0 41.2 %collective-permute-start.26 = (bf16[2304,512]{1,0:T(8,128)(2,1)}, bf16[2304,512]{1,0:T(8,128)(2,1)}, u32[]{:S(2)}, u32[]{:S(2)}) collective-permute-start(bf16[2304,512]{1,0:T(8,128)(2,1)} %across_2.1.refs_6_), channel_id=1, source_target_pairs={{0,1},{1,0},{2,3},{3,2},{4,5},{5,4},{6,7},{7,6},{8,9},{9,8},{10,11... | collective-permute-start | bytes 7077896 | tf_op jit(solution)/shard_map/ppermute | solution.py:32
  198.0 32.4 %collective-permute-start.29 = (bf16[2304,512]{1,0:T(8,128)(2,1)}, bf16[2304,512]{1,0:T(8,128)(2,1)}, u32[]{:S(2)}, u32[]{:S(2)}) collective-permute-start(bf16[2304,512]{1,0:T(8,128)(2,1)} %across_3.1.refs_6_), channel_id=1, source_target_pairs={{0,1},{1,0},{2,3},{3,2},{4,5},{5,4},{6,7},{7,6},{8,9},{9,8},{10,11... | collective-permute-start | bytes 7077896 | tf_op jit(solution)/shard_map/ppermute | solution.py:32
  198.1 24.4 %collective-permute-start.25 = (bf16[864,512]{1,0:T(8,128)(2,1)}, bf16[864,512]{1,0:T(8,128)(2,1)}, u32[]{:S(2)}, u32[]{:S(2)}) collective-permute-start(bf16[864,512]{1,0:T(8,128)(2,1)} %get-tuple-element.146), channel_id=1, source_target_pairs={{0,8},{1,9},{2,10},{3,11},{4,12},{5,13},{6,14},{7,15},{8,0},{9,1},... | collective-permute-start | bytes 2654216 | tf_op jit(solution)/shard_map/ppermute | solution.py:32
  199.8 22.7 %collective-permute-start.24 = (bf16[864,512]{1,0:T(8,128)(2,1)}, bf16[864,512]{1,0:T(8,128)(2,1)}, u32[]{:S(2)}, u32[]{:S(2)}) collective-permute-start(bf16[864,512]{1,0:T(8,128)(2,1)} %get-tuple-element.145.refs_5_), channel_id=1, source_target_pairs={{0,4},{1,5},{2,6},{3,7},{4,0},{5,1},{6,2},{7,3},{8,12},{9,13},{10,... | collective-permute-start | bytes 2654216 | tf_op jit(solution)/shard_map/ppermute | solution.py:32
  225.2 28.2 %collective-permute-start.27 = (bf16[576,512]{1,0:T(8,128)(2,1)}, bf16[576,512]{1,0:T(8,128)(2,1)}, u32[]{:S(2)}, u32[]{:S(2)}) collective-permute-start(bf16[576,512]{1,0:T(8,128)(2,1)} %get-tuple-element.153), channel_id=1, source_target_pairs={{0,8},{1,9},{2,10},{3,11},{4,12},{5,13},{6,14},{7,15},{8,0},{9,1},... | collective-permute-start | bytes 1769480 | tf_op jit(solution)/shard_map/ppermute | solution.py:32
  225.8 27.6 %collective-permute-start.28 = (bf16[576,512]{1,0:T(8,128)(2,1)}, bf16[576,512]{1,0:T(8,128)(2,1)}, u32[]{:S(2)}, u32[]{:S(2)}) collective-permute-start(bf16[576,512]{1,0:T(8,128)(2,1)} %get-tuple-element.154.refs_5_), channel_id=1, source_target_pairs={{0,4},{1,5},{2,6},{3,7},{4,0},{5,1},{6,2},{7,3},{8,12},{9,13},{10,... | collective-permute-start | bytes 1769480 | tf_op jit(solution)/shard_map/ppermute | solution.py:32
  230.3 27.9 %collective-permute-start.31 = (bf16[2304,512]{1,0:T(8,128)(2,1)}, bf16[2304,512]{1,0:T(8,128)(2,1)}, u32[]{:S(2)}, u32[]{:S(2)}) collective-permute-start(bf16[2304,512]{1,0:T(8,128)(2,1)} %across_4.1.refs_6_), channel_id=1, source_target_pairs={{0,1},{1,0},{2,3},{3,2},{4,5},{5,4},{6,7},{7,6},{8,9},{9,8},{10,11... | collective-permute-start | bytes 7077896 | tf_op jit(solution)/shard_map/ppermute | solution.py:32
  257.2 24.3 %collective-permute-start.30 = (bf16[2304,512]{1,0:T(8,128)(2,1)}, bf16[2304,512]{1,0:T(8,128)(2,1)}, u32[]{:S(2)}, u32[]{:S(2)}) collective-permute-start(bf16[2304,512]{1,0:T(8,128)(2,1)} %across_5.1.refs_6_), channel_id=1, source_target_pairs={{0,1},{1,0},{2,3},{3,2},{4,5},{5,4},{6,7},{7,6},{8,9},{9,8},{10,11... | collective-permute-start | bytes 7077896 | tf_op jit(solution)/shard_map/ppermute | solution.py:32
  257.8 47.1 %collective-permute-start.32 = (bf16[2,16,768]{2,1,0:T(8,128)(2,1)}, bf16[2,16,768]{2,1,0:T(8,128)(2,1)}, u32[]{:S(2)}, u32[]{:S(2)}) collective-permute-start(bf16[2,16,768]{2,1,0:T(8,128)(2,1)} %get-tuple-element.172), channel_id=1, source_target_pairs={{0,1},{1,0},{2,3},{3,2},{4,5},{5,4},{6,7},{7,6},{8,9},{9,8},{10,11... | collective-permute-start | bytes 147464 | tf_op jit(solution)/shard_map/ppermute | solution.py:32
  257.8 47.0 %collective-permute-start.33 = (bf16[2,16,768]{2,1,0:T(8,128)(2,1)}, bf16[2,16,768]{2,1,0:T(8,128)(2,1)}, u32[]{:S(2)}, u32[]{:S(2)}) collective-permute-start(bf16[2,16,768]{2,1,0:T(8,128)(2,1)} %get-tuple-element.173), channel_id=1, source_target_pairs={{0,1},{1,0},{2,3},{3,2},{4,5},{5,4},{6,7},{7,6},{8,9},{9,8},{10,11... | collective-permute-start | bytes 147464 | tf_op jit(solution)/shard_map/ppermute | solution.py:32
  281.4 23.5 %collective-permute-start.34 = (bf16[2,16,768]{2,1,0:T(8,128)(2,1)}, bf16[2,16,768]{2,1,0:T(8,128)(2,1)}, u32[]{:S(2)}, u32[]{:S(2)}) collective-permute-start(bf16[2,16,768]{2,1,0:T(8,128)(2,1)} %get-tuple-element.174), channel_id=1, source_target_pairs={{0,1},{1,0},{2,3},{3,2},{4,5},{5,4},{6,7},{7,6},{8,9},{9,8},{10,11... | collective-permute-start | bytes 147464 | tf_op jit(solution)/shard_map/ppermute | solution.py:32
  307.3 15.5 %collective-permute-start.36 = (bf16[16,2432]{1,0:T(8,128)(2,1)}, bf16[16,2432]{1,0:T(8,128)(2,1)}, u32[]{:S(2)}, u32[]{:S(2)}) collective-permute-start(bf16[16,2432]{1,0:T(8,128)(2,1)} %get-tuple-element.181), channel_id=1, source_target_pairs={{0,2},{1,3},{2,0},{3,1},{4,6},{5,7},{6,4},{7,5},{8,10},{9,11},{10,... | collective-permute-start | bytes 233480 | tf_op jit(solution)/shard_map/ppermute | solution.py:32
  324.4 93.2 %all-gather.5.cloned.1.call-start = ((), (), s32[]{:S(2)}) async-start(), calls=%async_computation.1 | async-start | bytes 1622016 | tf_op jit(solution)/shard_map/all_gather | solution.py:1298
  324.4 37.5 %collective-permute-start.35 = (bf16[256,1536]{1,0:T(8,128)(2,1)}, bf16[256,1536]{1,0:T(8,128)(2,1)}, u32[]{:S(2)}, u32[]{:S(2)}) collective-permute-start(bf16[256,1536]{1,0:T(8,128)(2,1)} %get-tuple-element.178), channel_id=1, source_target_pairs={{0,2},{1,3},{2,0},{3,1},{4,6},{5,7},{6,4},{7,5},{8,10},{9,11},{10,... | collective-permute-start | bytes 2359304 | tf_op jit(solution)/shard_map/ppermute | solution.py:32
  330.2 16.1 %collective-permute-start.40 = (bf16[16,2816]{1,0:T(8,128)(2,1)}, bf16[16,2816]{1,0:T(8,128)(2,1)}, u32[]{:S(2)}, u32[]{:S(2)}) collective-permute-start(bf16[16,2816]{1,0:T(8,128)(2,1)} %get-tuple-element.189.rest_1_), channel_id=1, source_target_pairs={{0,2},{1,3},{2,0},{3,1},{4,6},{5,7},{6,4},{7,5},{8,10},{9,11},{10,... | collective-permute-start | bytes 270344 | tf_op jit(solution)/shard_map/ppermute | solution.py:32
  348.0 14.6 %collective-permute-start.37 = (bf16[2,4,512,128]{3,2,1,0:T(8,128)(2,1)}, bf16[2,4,512,128]{3,2,1,0:T(8,128)(2,1)}, u32[]{:S(2)}, u32[]{:S(2)}) collective-permute-start(bf16[2,4,512,128]{3,2,1,0:T(8,128)(2,1)} %get-tuple-element.184), channel_id=1, source_target_pairs={{0,1},{1,0},{2,3},{3,2},{4,5},{5,4},{6,7},{7,6},{8,9},{9,8},{10,11... | collective-permute-start | bytes 3145736 | tf_op jit(solution)/shard_map/ppermute | solution.py:32
  362.0 3.3 collective-permute-start.41
  379.9 4.7 %collective-permute-start.43 = (bf16[16,2048]{1,0:T(8,128)(2,1)}, bf16[16,2048]{1,0:T(8,128)(2,1)}, u32[]{:S(2)}, u32[]{:S(2)}) collective-permute-start(bf16[16,2048]{1,0:T(8,128)(2,1)} %get-tuple-element.201), channel_id=1, source_target_pairs={{0,2},{1,3},{2,0},{3,1},{4,6},{5,7},{6,4},{7,5},{8,10},{9,11},{10,... | collective-permute-start | bytes 196616 | tf_op jit(solution)/shard_map/ppermute | solution.py:32
  386.2 19.5 %collective-permute-start.46 = (bf16[32,2048]{1,0:T(8,128)(2,1)}, bf16[32,2048]{1,0:T(8,128)(2,1)}, u32[]{:S(2)}, u32[]{:S(2)}) collective-permute-start(bf16[32,2048]{1,0:T(8,128)(2,1)} %join.8.refs_11_.refs_0_), channel_id=1, source_target_pairs={{0,24},{1,25},{2,26},{3,27},{4,28},{5,29},{6,30},{7,31},{8,16},{9,... | collective-permute-start | bytes 393224 | tf_op jit(solution)/shard_map/ppermute | solution.py:32
  389.7 20.4 %collective-permute-start.45 = (bf16[32,2048]{1,0:T(8,128)(2,1)}, bf16[32,2048]{1,0:T(8,128)(2,1)}, u32[]{:S(2)}, u32[]{:S(2)}) collective-permute-start(bf16[32,2048]{1,0:T(8,128)(2,1)} %join.8.refs_11_.refs_0_), channel_id=1, source_target_pairs={{0,16},{1,17},{2,18},{3,19},{4,20},{5,21},{6,22},{7,23},{8,24},{9,... | collective-permute-start | bytes 393224 | tf_op jit(solution)/shard_map/ppermute | solution.py:32
  389.7 20.4 %collective-permute-start.44 = (bf16[32,2048]{1,0:T(8,128)(2,1)}, bf16[32,2048]{1,0:T(8,128)(2,1)}, u32[]{:S(2)}, u32[]{:S(2)}) collective-permute-start(bf16[32,2048]{1,0:T(8,128)(2,1)} %join.8.refs_11_.refs_0_), channel_id=1, source_target_pairs={{0,8},{1,9},{2,10},{3,11},{4,12},{5,13},{6,14},{7,15},{8,0},{9,1},... | collective-permute-start | bytes 393224 | tf_op jit(solution)/shard_map/ppermute | solution.py:32
  412.1 15.8 %collective-permute-start.47 = (bf16[256,1536]{1,0:T(8,128)(2,1)}, bf16[256,1536]{1,0:T(8,128)(2,1)}, u32[]{:S(2)}, u32[]{:S(2)}) collective-permute-start(bf16[256,1536]{1,0:T(8,128)(2,1)} %gate.5), channel_id=1, source_target_pairs={{0,2},{1,3},{2,0},{3,1},{4,6},{5,7},{6,4},{7,5},{8,10},{9,11},{10,... | collective-permute-start | bytes 2359304 | tf_op jit(solution)/shard_map/ppermute | solution.py:32
  413.9 9.6 %collective-permute-start.48 = (bf16[128,2048]{1,0:T(8,128)(2,1)}, bf16[128,2048]{1,0:T(8,128)(2,1)}, u32[]{:S(2)}, u32[]{:S(2)}) collective-permute-start(bf16[128,2048]{1,0:T(8,128)(2,1)} %join.9.refs_1_.refs_0_), channel_id=1, source_target_pairs={{0,4},{1,5},{2,6},{3,7},{4,0},{5,1},{6,2},{7,3},{8,12},{9,13},{10,... | collective-permute-start | bytes 1572872 | tf_op jit(solution)/shard_map/ppermute | solution.py:32
  (3 other events, 5.3 us)
Sparse Core Ops, SparseCore 0:
  324.5 42.4 all-gather.2
  369.8 43.1 all-gather.4
